TPU v7x, 128 devices: a whole 4x4x4 slice. The times are simulated.
128 devices in a mesh: prow: 8 (over z, core), pcol: 16 (over y, x).
Axes of the slice: x: 4, y: 4, z: 4, core: 2. Of those that a mesh axis runs over, the one named last changes fastest.
Arguments:
- ancestor_inv: float32 [16384, 16384], P('prow', 'pcol'), as said below
- lhat_parent: float32 [16384, 512], P('pcol'), may hold values from -0.09375 to 0.09375
- lhat_child: float32 [16384, 512], P('pcol'), may hold values from -0.09375 to 0.09375
- lhat_cross: float32 [512, 512], replicated, may hold values from -0.25 to 0.25
- diag_parent: float32 [512, 512], replicated, as said below
- diag_child: float32 [512, 512], replicated, as said below
- structure: int32 [2, 64], replicated, may hold values from 0 to 1, as said below
- widths: int32 [2], replicated, may hold values from 64 to 512, as said below
Outputs:
- inv_sp: float32 [16384, 512], P('pcol')
- inv_pp: float32 [512, 512], replicated
- inv_sc: float32 [16384, 512], P('pcol')
- inv_pc: float32 [512, 512], replicated
- inv_cc: float32 [512, 512], replicated
Inputs may be any that keep to these rules, and one draw needn't show every extreme that they name: ancestor_inv is exactly symmetric: the identity plus a symmetric part whose entries are of order 1 / sqrt(16384). diag_parent is exactly symmetric: 1.5 times the identity plus a symmetric part whose entries are of order 1 / sqrt(512). diag_child is exactly symmetric: 1.5 times the identity plus a symmetric part whose entries are of order 1 / sqrt(512). `structure`: 0 or 1; every block in the child's structure is in the parent's. `widths`: one of the two equals 512.
All inputs are finite; a program needn't handle non-finite values.
Results may differ from a plain program's by a relative error of at most 0.000073.
Values sent between devices are 32-bit elements; how exact they have to be, the bound alone decides.
No kernel may reach another device: no remote copies, remote signals or barrier semaphores. Data moves between devices by JAX's collectives and lax.ppermute only.
A program may use at most 128 MiB of HBM per device.

v0:
```python
import functools

import jax
import jax.numpy as jnp
from jax import lax
from jax.experimental import pallas as pl
from jax.experimental.pallas import tpu as pltpu
from jax.sharding import PartitionSpec as P

BLK = 256
AXES = ("prow", "pcol")
SIDE = 4
LANES = 128
MIB = 1 << 20
SPAN = range(SIDE)
CHUNKS = 2 * SIDE
SLICE = 16
GROUP = SIDE * SLICE
CAPACITIES = (36, 46, 64)
BUCKET, TURNED, PLANE_Z, CORE, OUTER = range(5)
OWN, ROW, WIDTHS, DEST, PLAN_SIZE = 16, 48, 112, 114, 128


def flat(z, k, y, x):
    return ((z % SIDE) * 2 + k) * SIDE * SIDE + (y % SIDE) * SIDE + x % SIDE


PLACES = [(z, k, y, x) for z in SPAN for k in (0, 1) for y in SPAN for x in SPAN]
ROWS_OF_CORE_0 = [[flat(z, 0, y, x) for x in SPAN] for z in SPAN for y in SPAN]
COLS_OF_CORE_0 = [[flat(z, 0, y, x) for y in SPAN] for z in SPAN for x in SPAN]
ROWS_OF_CORE_1 = [[flat(z, 1, y, x) for x in SPAN] for z in SPAN for y in SPAN]
COLS_OF_CORE_1 = [[flat(z, 1, y, x) for y in SPAN] for z in SPAN for x in SPAN]
NEAR = ROWS_OF_CORE_0 + COLS_OF_CORE_1
FAR = COLS_OF_CORE_0 + ROWS_OF_CORE_1
STACK = [[flat(z, k, y, x) for z in SPAN] for k in (0, 1) for y in SPAN for x in SPAN]
STACK = [[flat(z, k, y, x) for z in SPAN] for k in (0, 1) for y in SPAN for x in SPAN]
PLANE = [[flat(z, 0, y, x) for y in SPAN for x in SPAN] for z in SPAN] + [
    [flat(z, 1, y, x) for x in SPAN for y in SPAN] for z in SPAN
]


def piece_of(k, y, x):
    return SIDE * y + x if k == 0 else SIDE * x + y


def deals():
    pairs, slices, turned, used = [[], []], [[0] * 128, [0] * 128], [0] * 128, {}
    for z, k, y, x in PLACES:
        here, p = flat(z, k, y, x), piece_of(k, y, x)
        near = x // 2
        turned[here] = near
        for i, block in enumerate((near, 1 - near)):
            plane = (z + y + 2 * k) % SIDE
            core = used.get((i, z, k, block, plane), 0)
            used[i, z, k, block, plane] = core + 1
            there = flat(plane, core, z, 2 * k + block)
            pairs[i].append((there, here))
            slices[i][there] = p
    rows = [[here // 16, here % 16, slices[0][here], slices[1][here], turned[here]] for here in range(128)]
    return pairs, rows


DEALS, PLACE_TABLE = deals()


def partner(z, k, near):
    return z ^ (1 if (k == 0) == near else 3)


def swap_planes(value, near):
    pairs = [(flat(partner(z, k, near), k, y, x), flat(z, k, y, x)) for z, k, y, x in PLACES]
    return lax.ppermute(value, AXES, pairs)


PLANE_ORDER = ((0, 3, 1, 2), (0, 1, 3, 2))


def plane_at(z, core, place):
    return z ^ jnp.where(core == 0, PLANE_ORDER[0][place], PLANE_ORDER[1][place])


def fetch_far(value, d):
    pairs = [(flat(z, k, y + d * (1 - k), x + d * k), flat(z, k, y, x)) for z, k, y, x in PLACES]
    return lax.ppermute(value, AXES, pairs)


def swap_cores(value):
    pairs = [(flat(z, 1 - k, y, x), flat(z, k, y, x)) for z, k, y, x in PLACES]
    return lax.ppermute(value, AXES, pairs)


def exchange(value, groups):
    return lax.all_to_all(value, AXES, 0, 0, axis_index_groups=groups, tiled=True)


def gather(value, groups):
    size = len(groups[0])
    return exchange(jnp.broadcast_to(value[None], (size,) + value.shape), groups)


def scatter_sum(value, groups):
    return jnp.sum(exchange(value, groups), axis=0)


def split(value):
    high = value.astype(jnp.bfloat16)
    return high, (value - high.astype(jnp.float32)).astype(jnp.bfloat16)


def dot3(left, right, dims=(((1,), (0,)), ((), ()))):
    left_high, left_low = split(left)
    right_high, right_low = split(right)

    def dot(a, b):
        return lax.dot_general(a, b, dims, preferred_element_type=jnp.float32)

    return dot(left_high, right_high) + (dot(left_high, right_low) + dot(left_low, right_high))


def split_transposed_kernel(a_ref, out_ref):
    @pl.loop(0, SIDE)
    def _(o):
        parts = [a_ref[pl.ds(pl.multiple_of(BLK * i + GROUP * o, GROUP), GROUP), :] for i in range(2)]
        high, low = split(jnp.concatenate(parts, axis=0))
        out_ref[o, 0] = high.T
        out_ref[o, 1] = low.T


def split_transposed(a):
    rows, cols = a.shape
    out = pl.BlockSpec((SIDE, 2, cols, 2 * GROUP), lambda i: (0, 0, 0, i))
    return pl.pallas_call(
        split_transposed_kernel,
        grid=(rows // (2 * BLK),),
        in_specs=[pl.BlockSpec((2 * BLK, cols), lambda i: (i, 0))],
        out_specs=out,
        out_shape=jax.ShapeDtypeStruct((SIDE, 2, cols, rows // SIDE), jnp.bfloat16),
        compiler_params=pltpu.CompilerParams(vmem_limit_bytes=50 * MIB),
        cost_estimate=pl.CostEstimate(flops=rows * cols, bytes_accessed=8 * rows * cols, transcendentals=0),
    )(a)


def smem(*shape):
    return pl.BlockSpec(memory_space=pltpu.SMEM)


def plan_kernel(place_ref, structure_ref, widths_ref, plan_ref, counts):
    r, c = place_ref[0], place_ref[1]
    chunks = [(widths_ref[i] + LANES - 1) // LANES for i in range(2)]

    def zero(i, _):
        plan_ref[i] = 0
        return 0

    lax.fori_loop(0, PLAN_SIZE, zero, 0)

    def count(col, _):
        total = jnp.int32(0)
        for b in range(4):
            for i in range(2):
                total += jnp.where(structure_ref[i, 4 * col + b] > 0, chunks[i], 0)
        counts[col] = total
        return 0

    lax.fori_loop(0, 16, count, 0)
    most_row = lax.fori_loop(0, 8, lambda i, m: jnp.maximum(m, counts[2 * i] + counts[2 * i + 1]), jnp.int32(0))
    bucket = jnp.int32(0)
    for slots in CAPACITIES[:-1]:
        bucket += jnp.where(most_row > slots, 1, 0)
    plan_ref[BUCKET] = bucket

    def mark(start, base, blocks):
        def one(b, run):
            for q in range(CHUNKS):
                active = (structure_ref[q // SIDE, start + b] > 0) & (q % SIDE < chunks[q // SIDE])
                plan_ref[base + b * CHUNKS + q] = jnp.where(active, run, -1)
                run += jnp.where(active, 1, 0)
            return run

        return lax.fori_loop(0, blocks, one, jnp.int32(0))

    mark(4 * c, OWN, 4)
    mark(8 * r, ROW, 8)
    plan_ref[TURNED] = place_ref[4]
    plan_ref[PLANE_Z] = r // 2
    core = lax.rem(r, 2)
    plan_ref[CORE] = core
    plan_ref[OUTER] = jnp.where(core == 0, c // SIDE, lax.rem(c, SIDE))
    for i in range(2):
        plan_ref[WIDTHS + i] = widths_ref[i]
    for q in range(CHUNKS):
        owner = (q % SIDE) // 2
        apart = (r // 2) ^ (2 * (q // SIDE) + q % 2)
        dest = jnp.int32(0)
        for n in range(1, SIDE):
            dest = jnp.where(apart == PLANE_ORDER[owner][n], n, dest)
        plan_ref[DEST + q] = dest + jnp.where(core == owner, 0, SIDE)


def make_plan(place, structure, widths):
    return pl.pallas_call(
        plan_kernel,
        in_specs=[smem()] * 3,
        out_specs=smem(),
        out_shape=jax.ShapeDtypeStruct((PLAN_SIZE,), jnp.int32),
        scratch_shapes=[pltpu.SMEM((16,), jnp.int32)],
    )(place, structure, widths)


def pack_kernel(place_ref, parent_a, parent_b, child_a, child_b, out_a, out_b):
    out_a[0], out_b[0] = parent_a[...], parent_b[...]
    out_a[1], out_b[1] = child_a[...], child_b[...]


def pack(place, parent, child):
    width = parent.shape[1]
    shaped = [panel.reshape(4, BLK, width) for panel in (parent, child)]
    specs = [pl.BlockSpec((4, SLICE, width), lambda i, place, at=at: (0, place[at], 0)) for at in (2, 3)]
    out = pl.BlockSpec((2, 4, SLICE, width), lambda i, place: (0, 0, 0, 0))
    return pl.pallas_call(
        pack_kernel,
        grid_spec=pltpu.PrefetchScalarGridSpec(
            num_scalar_prefetch=1, grid=(1,), in_specs=specs + specs, out_specs=[out, out]
        ),
        out_shape=[jax.ShapeDtypeStruct((2, 4, SLICE, width), jnp.float32)] * 2,
        compiler_params=pltpu.CompilerParams(vmem_limit_bytes=60 * MIB),
        cost_estimate=pl.CostEstimate(flops=0, bytes_accessed=MIB, transcendentals=0),
    )(place, shaped[0], shaped[0], shaped[1], shaped[1])


def merge_kernel(plan_ref, from_a, from_b, out_ref):
    turned = plan_ref[TURNED] > 0

    @pl.loop(0, 4)
    def _(b):
        for q in range(CHUNKS):
            cols = pl.ds(LANES * (q % SIDE), LANES)
            value_a, value_b = from_a[q // SIDE, b, :, cols], from_b[q // SIDE, b, :, cols]
            for half in range(2):
                slot = plan_ref[ROW + (4 * half + b) * CHUNKS + q]
                value = jnp.where(turned == (half == 0), value_b, value_a)

                @pl.when(slot >= 0)
                def _():
                    for i in SPAN:
                        out_ref[i, slot] = value


def merge(plan, from_a, from_b, slots):
    ins = pl.BlockSpec(from_a.shape, lambda i, plan: (0, 0, 0, 0))
    return pl.pallas_call(
        merge_kernel,
        grid_spec=pltpu.PrefetchScalarGridSpec(
            num_scalar_prefetch=1,
            grid=(1,),
            in_specs=[ins, ins],
            out_specs=pl.BlockSpec((SIDE, slots, SLICE, LANES), lambda i, plan: (0, 0, 0, 0)),
        ),
        out_shape=jax.ShapeDtypeStruct((SIDE, slots, SLICE, LANES), jnp.float32),
        compiler_params=pltpu.CompilerParams(vmem_limit_bytes=16 * MIB),
        cost_estimate=pl.CostEstimate(flops=0, bytes_accessed=4 * MIB, transcendentals=0),
    )(plan, from_a, from_b)


def product_kernel(sizes, has_earlier, plan_ref, *refs):
    count = len(sizes)
    tiles, refs = refs[:count], refs[count:]
    pieces, refs = refs[: sum(sizes)], refs[sum(sizes) :]
    out_refs, (panel_high, panel_low) = refs[has_earlier:-2], refs[-2:]
    tile, depth = tiles[0].shape[2:]

    @pl.when(pl.program_id(0) == 0)
    def _():
        @pl.loop(0, depth // GROUP)
        def _(b):
            for q in range(CHUNKS):
                slot = plan_ref[ROW + b * CHUNKS + q]
                lane = lax.broadcasted_iota(jnp.int32, (GROUP, LANES), 1) + LANES * (q % SIDE)
                kept, slot = (lane < plan_ref[WIDTHS + q // SIDE]) & (slot >= 0), jnp.maximum(slot, 0)
                cols = pl.ds(pl.multiple_of(LANES * plan_ref[DEST + q], LANES), LANES)
                first = 0
                for g, size in enumerate(sizes):
                    values = [ref[:, slot].reshape(-1, LANES) for ref in pieces[first : first + size]]
                    first += size
                    value = values[0] if size == 1 else jnp.concatenate(values, axis=0)
                    high, low = split(jnp.where(kept, value, 0.0))
                    rows = pl.ds(pl.multiple_of(GROUP * b + depth * g, GROUP), GROUP)
                    panel_high[rows, cols] = high
                    panel_low[rows, cols] = low

    width = SIDE * LANES

    def half(i):
        cols = pl.ds(width * i, width) if isinstance(i, int) else pl.ds(pl.multiple_of(width * i, width), width)
        total = None
        for g in range(count):
            rows = pl.ds(depth * g, depth)
            both = tiles[g][0].reshape(2 * tile, depth)
            part = jnp.dot(both, panel_high[rows, cols], preferred_element_type=jnp.float32)
            part = part[:tile] + part[tile:]
            part += jnp.dot(tiles[g][0, 0], panel_low[rows, cols], preferred_element_type=jnp.float32)
            total = part if total is None else total + part
        return [total[:, LANES * q : LANES * (q + 1)] for q in SPAN]

    if len(out_refs) == 1:

        @pl.loop(0, 2)
        def _(i):
            for q, value in enumerate(half(i)):
                out_refs[0][SIDE * i + q] = value + refs[0][SIDE * i + q] if has_earlier else value
    else:
        for i in range(2):
            for q, value in enumerate(half(i)):
                out_refs[2 * i + q // 2][q % 2] = value + refs[0][SIDE * i + q]


def product(plan, split_tile, shifts, groups, earlier=None, is_last=False):
    _, _, cols, depth = split_tile.shape
    tile = 256
    pieces = [piece for group in groups for piece in group]
    whole = pl.BlockSpec((CHUNKS, tile, LANES), lambda i, plan: (0, i, 0))
    pair = pl.BlockSpec((2, tile, LANES), lambda i, plan: (0, i, 0))
    tiles = [
        pl.BlockSpec(
            (1, 2, tile, depth), lambda i, plan, shift=shift: (lax.rem(plan[OUTER] + shift, SIDE), 0, i, 0))
        for shift in shifts
    ]
    kernel = functools.partial(product_kernel, [len(group) for group in groups], earlier is not None)
    return pl.pallas_call(
        kernel,
        grid_spec=pltpu.PrefetchScalarGridSpec(
            num_scalar_prefetch=1,
            grid=(cols // tile,),
            in_specs=tiles
            + [pl.BlockSpec(piece.shape, lambda i, plan: (0, 0, 0, 0)) for piece in pieces]
            + [whole] * (earlier is not None),
            out_specs=[pair] * 4 if is_last else whole,
            scratch_shapes=[pltpu.VMEM((depth * len(shifts), CHUNKS * LANES), jnp.bfloat16)] * 2,
        ),
        out_shape=[jax.ShapeDtypeStruct((2, cols, LANES), jnp.float32)] * 4
        if is_last
        else jax.ShapeDtypeStruct((CHUNKS, cols, LANES), jnp.float32),
        compiler_params=pltpu.CompilerParams(vmem_limit_bytes=32 * MIB),
        cost_estimate=pl.CostEstimate(
            flops=6 * len(shifts) * depth * cols * CHUNKS * LANES, bytes_accessed=12 * MIB, transcendentals=0
        ),
    )(plan, *[split_tile] * len(shifts), *pieces, *([] if earlier is None else [earlier]))


def products(slots):
    def run(plan, split_tile, dealt):
        near = exchange(merge(plan, *dealt, slots), NEAR)
        ahead, behind = fetch_far(near, 1), fetch_far(near, 3)
        total = product(plan, split_tile, (0,), ((near,),))
        total, ahead, behind = lax.optimization_barrier((total, ahead, behind))
        far_first, far_last = fetch_far(ahead[:2], 1), fetch_far(behind[2:], 3)
        total = product(plan, split_tile, (1, 3), ((ahead,), (behind,)), total)
        return product(plan, split_tile, (2,), ((far_first, far_last),), total, True)

    return run


def turn_kernel(plan_ref, parent_ref, child_ref, high_ref, low_ref):
    first = slab_chunk(plan_ref[PLANE_Z], plan_ref[CORE])
    t = pl.program_id(0)
    q = lax.rem(first + t, CHUNKS)
    lane = lax.broadcasted_iota(jnp.int32, (BLK, LANES), 1)
    for panel, ref in enumerate((parent_ref, child_ref)):

        @pl.when(q // SIDE == panel)
        def _():
            start = LANES * lax.rem(q, SIDE)
            cols = pl.ds(pl.multiple_of(start, LANES), LANES)
            mask = jnp.where(lane + start < plan_ref[WIDTHS + panel], 1.0, 0.0)
            for b in range(4):
                keep = jnp.where(plan_ref[OWN + b * CHUNKS + SIDE * panel] >= 0, 1.0, 0.0)
                rows = pl.ds(BLK * b, BLK)
                high, low = split(ref[rows, cols] * mask * keep)
                high_ref[:, rows] = high.T
                low_ref[:, rows] = low.T


def turn(plan, parent, child):
    rows, width = parent.shape
    out = pl.BlockSpec((LANES, rows), lambda t, plan: (t, 0))
    panel = pl.BlockSpec((rows, width), lambda t, plan: (0, 0))
    return pl.pallas_call(
        turn_kernel,
        grid_spec=pltpu.PrefetchScalarGridSpec(
            num_scalar_prefetch=1, grid=(5,), in_specs=[panel, panel], out_specs=[out, out]
        ),
        out_shape=[jax.ShapeDtypeStruct((5 * LANES, rows), jnp.bfloat16)] * 2,
        compiler_params=pltpu.CompilerParams(vmem_limit_bytes=48 * MIB),
        cost_estimate=pl.CostEstimate(flops=MIB, bytes_accessed=8 * MIB, transcendentals=0),
    )(plan, parent, child)


def slab_kernel(kept_ref, passed_ref, high_ref, low_ref, slab_ref, sums_ref):
    slab = kept_ref[...] + passed_ref[...]
    slab_ref[...] = slab
    slab_high, slab_low = split(slab)
    total = jnp.dot(high_ref[...], slab_high, preferred_element_type=jnp.float32)
    total += jnp.dot(high_ref[...], slab_low, preferred_element_type=jnp.float32)
    sums_ref[...] = total + jnp.dot(low_ref[...], slab_high, preferred_element_type=jnp.float32)


def finish_slab(kept, passed, high, low):
    rows, width = kept.shape
    return pl.pallas_call(
        slab_kernel,
        out_shape=[
            jax.ShapeDtypeStruct((rows, width), jnp.float32),
            jax.ShapeDtypeStruct((high.shape[0], width), jnp.float32),
        ],
        compiler_params=pltpu.CompilerParams(vmem_limit_bytes=16 * MIB),
        cost_estimate=pl.CostEstimate(flops=6 * high.size * width, bytes_accessed=6 * MIB, transcendentals=0),
    )(kept, passed, high, low)


def slab_chunk(z, k):
    return SIDE * (z // 2) + 2 * k + lax.rem(z, 2)


def masked_cross(plan_ref, cross_ref):
    rows = lax.broadcasted_iota(jnp.int32, cross_ref.shape, 0)
    cols = lax.broadcasted_iota(jnp.int32, cross_ref.shape, 1)
    keep = jnp.where(rows < plan_ref[WIDTHS], 1.0, 0.0) * jnp.where(cols < plan_ref[WIDTHS + 1], 1.0, 0.0)
    return cross_ref[...] * keep


def masked_square(ref, width):
    rows = lax.broadcasted_iota(jnp.int32, ref.shape, 0)
    cols = lax.broadcasted_iota(jnp.int32, ref.shape, 1)
    return ref[...] * (jnp.where(rows < width, 1.0, 0.0) * jnp.where(cols < width, 1.0, 0.0))


def rows_kernel(plan_ref, own_a, own_b, other_a, other_b, cross_ref, inv_sp_ref, inv_sc_ref, total):
    z, k = plan_ref[PLANE_Z], plan_ref[CORE]
    for refs, core in (((own_a, own_b), k), ((other_a, other_b), 1 - k)):
        for i in SPAN:
            start = LANES * slab_chunk(plane_at(z, core, i), core)
            total[:, pl.ds(pl.multiple_of(start, LANES), LANES)] = refs[i // 2][i % 2]
    width = cross_ref.shape[0]
    block = OWN + pl.program_id(0) * CHUNKS
    keep = [jnp.where(plan_ref[block + SIDE * i] >= 0, 1.0, 0.0) for i in range(2)]
    inv_sp = -total[:, :width] * keep[0]
    inv_sp_ref[...] = inv_sp
    inv_sc_ref[...] = -(total[:, width:] + dot3(inv_sp, masked_cross(plan_ref, cross_ref))) * keep[1]


def finish_rows(plan, slabs, cross):
    _, rows, _ = slabs[0].shape
    width = cross.shape[0]
    pair = pl.BlockSpec((2, BLK, LANES), lambda i, plan: (0, i, 0))
    whole = pl.BlockSpec((BLK, width), lambda i, plan: (i, 0))
    return pl.pallas_call(
        rows_kernel,
        grid_spec=pltpu.PrefetchScalarGridSpec(
            num_scalar_prefetch=1,
            grid=(rows // BLK,),
            in_specs=[pair] * 4 + [pl.BlockSpec((width, width), lambda i, plan: (0, 0))],
            out_specs=[whole, whole],
            scratch_shapes=[pltpu.VMEM((BLK, 2 * width), jnp.float32)],
        ),
        out_shape=[jax.ShapeDtypeStruct((rows, width), jnp.float32)] * 2,
        compiler_params=pltpu.CompilerParams(vmem_limit_bytes=32 * MIB),
        cost_estimate=pl.CostEstimate(flops=6 * rows * width * width, bytes_accessed=16 * rows * width, transcendentals=0),
    )(plan, *slabs, cross)


def blocks_kernel(
    plan_ref, own_ref, other_ref, cross_ref, parent_ref, child_ref, inv_pp_ref, inv_pc_ref, inv_cc_ref, slab, total
):
    share = own_ref.shape[2]
    k = plan_ref[CORE]
    for ref, core in ((own_ref, k), (other_ref, 1 - k)):
        for z in SPAN:
            j = SIDE * (z // 2) + 2 * core + z % 2
            for i in SPAN:
                slab[j, pl.ds(share * i, share), :] = ref[i, z]
    for j in range(CHUNKS):
        for i in range(CHUNKS):
            t = (i - j) % CHUNKS
            if t <= 4:
                block = slab[j, pl.ds(LANES * t, LANES), :]
            else:
                block = slab[i, pl.ds(LANES * (CHUNKS - t), LANES), :].T
            total[pl.ds(LANES * i, LANES), pl.ds(LANES * j, LANES)] = block
    width = cross_ref.shape[0]
    cross = masked_cross(plan_ref, cross_ref)
    inv_pp = masked_square(parent_ref, plan_ref[WIDTHS]) + total[:width, :width]
    inv_pp_ref[...] = inv_pp
    inv_pc = total[:width, width:] - dot3(inv_pp, cross)
    inv_pc_ref[...] = inv_pc
    last = dot3(cross, inv_pc, (((0,), (0,)), ((), ()))) + dot3(total[width:, :width], cross)
    inv_cc_ref[...] = masked_square(child_ref, plan_ref[WIDTHS + 1]) + total[width:, width:] - last


def finish_blocks(plan, own, other, cross, parent, child):
    width = cross.shape[0]
    square = pl.BlockSpec((width, width), lambda i, plan: (0, 0))
    sums = pl.BlockSpec(own.shape, lambda i, plan: (0, 0, 0, 0))
    return pl.pallas_call(
        blocks_kernel,
        grid_spec=pltpu.PrefetchScalarGridSpec(
            num_scalar_prefetch=1,
            grid=(1,),
            in_specs=[sums, sums] + [square] * 3,
            out_specs=[square] * 3,
            scratch_shapes=[
                pltpu.VMEM((CHUNKS, 5 * LANES, LANES), jnp.float32),
                pltpu.VMEM((2 * width, 2 * width), jnp.float32),
            ],
        ),
        out_shape=[jax.ShapeDtypeStruct((width, width), jnp.float32)] * 3,
        compiler_params=pltpu.CompilerParams(vmem_limit_bytes=32 * MIB),
        cost_estimate=pl.CostEstimate(flops=18 * width**3, bytes_accessed=40 * width * width, transcendentals=0),
    )(plan, own, other, cross, parent, child)


def per_device(
    ancestor_inv, lhat_parent, lhat_child, lhat_cross, diag_parent, diag_child, structure, widths
):
    here = lax.axis_index("prow") * 16 + lax.axis_index("pcol")
    place = lax.dynamic_index_in_dim(jnp.array(PLACE_TABLE, jnp.int32), here, 0, keepdims=False)
    sent = pack(place, lhat_parent, lhat_child)
    dealt = [lax.ppermute(value, AXES, pairs) for value, pairs in zip(sent, DEALS)]
    plan, split_tile, *dealt = lax.optimization_barrier(
        (make_plan(place, structure, widths), split_transposed(ancestor_inv), *dealt))
    kept, passed, send_kept, send_passed = lax.switch(
        plan[BUCKET], [products(slots) for slots in CAPACITIES], plan, split_tile, dealt)

    passed = swap_planes(passed + swap_cores(send_passed), True)
    kept = kept + swap_cores(send_kept)
    kept, passed, high, low = lax.optimization_barrier((kept, passed, *turn(plan, lhat_parent, lhat_child)))
    kept = kept + passed
    slab, sums = finish_slab(kept[0], swap_planes(kept[1], False), high, low)

    far_slab = swap_planes(slab, False)
    sums = scatter_sum(sums.reshape(SIDE, -1, LANES), NEAR)
    far_slab, sums = lax.optimization_barrier((far_slab, sums))
    first = jnp.stack([slab, far_slab])
    second, other_first = swap_planes(first, True), swap_cores(first)
    sums = jnp.sum(gather(sums, FAR), axis=0)
    sums = gather(sums, STACK)
    second, other_first, sums = lax.optimization_barrier((second, other_first, sums))
    other_second = swap_cores(second)
    sums = gather(sums, NEAR)
    other_second, sums = lax.optimization_barrier((other_second, sums))
    other_sums = swap_cores(sums)
    inv_sp, inv_sc = finish_rows(plan, (first, second, other_first, other_second), lhat_cross)
    inv_sp, inv_sc, other_sums = lax.optimization_barrier((inv_sp, inv_sc, other_sums))
    inv_pp, inv_pc, inv_cc = finish_blocks(plan, sums, other_sums, lhat_cross, diag_parent, diag_child)
    return (inv_sp, inv_pp, inv_sc, inv_pc, inv_cc)


def solution(mesh):
    return jax.shard_map(
        per_device,
        mesh=mesh,
        in_specs=(P("prow", "pcol"), P("pcol", None), P("pcol", None), P(), P(), P(), P(), P()),
        out_specs=(P("pcol", None), P(), P("pcol", None), P(), P()),
        check_vma=False,
    )
```

profile of v0, /device:TPU:1, one launch (start us, length us, event | category | flops | bytes accessed | tf_op | source)
XLA Modules:
  0.0 175.6 jit_solution(4594164015260494339)
XLA Ops:
  0.6 1.2 dynamic-slice_bitcast_fusion.place_ref
  1.8 2.6 %shard_map.130 = (f32[2,4,16,512]{3,2,1,0:T(8,128)}, f32[2,4,16,512]{3,2,1,0:T(8,128)}) custom-call(s32[5]{0:T(128)} %dynamic-slice_bitcast_fusion.place_ref, f32[4,256,512]{2,1,0:T(8,128)} %bitcast.13, f32[4,256,512]{2,1,0:T(8,128)} %bitcast.14, f32[4,256,512]{2,1,0:T(8,128)} %bitcast.17, f32[4,256,512]{2,1,0:T(8,128)} %bitcast.18), custom_call_target="tpu_custom_call" | custom-call | bytes 1048576 | tf_op jit(solution)/shard_map/pallas_call | solution.py:220
  4.4 4.5 %collective-permute-start.12 = (f32[2,4,16,512]{3,2,1,0:T(8,128)}, f32[2,4,16,512]{3,2,1,0:T(8,128)S(1)}, u32[]{:S(2)}, u32[]{:S(2)}) collective-permute-start(f32[2,4,16,512]{3,2,1,0:T(8,128)} %get-tuple-element.83), channel_id=1, source_target_pairs={{0,0},{16,1},{1,2},{17,3},{32,4},{48,5},{33,6},{49,7},{64,8},{80,9... | collective-permute-start | bytes 786440 | tf_op jit(solution)/shard_map/ppermute | solution.py:527
  8.9 4.2 %collective-permute-start.13 = (f32[2,4,16,512]{3,2,1,0:T(8,128)}, f32[2,4,16,512]{3,2,1,0:T(8,128)S(1)}, u32[]{:S(2)}, u32[]{:S(2)}) collective-permute-start(f32[2,4,16,512]{3,2,1,0:T(8,128)} %get-tuple-element.84), channel_id=1, source_target_pairs={{1,0},{17,1},{0,2},{16,3},{33,4},{49,5},{32,6},{48,7},{65,8},{81,9... | collective-permute-start | bytes 786440 | tf_op jit(solution)/shard_map/ppermute | solution.py:527
  13.2 2.9 %shard_map.128.plan_ref = s32[128]{0:T(128)S(1)} custom-call(s32[5]{0:T(128)} %dynamic-slice_bitcast_fusion.place_ref, s32[2,64]{1,0:T(2,128)} %structure_ref.1, s32[2]{0:T(128)} %widths_ref.1), custom_call_target="tpu_custom_call" | custom-call | tf_op jit(solution)/shard_map/pallas_call | solution.py:201
  16.0 0.0 copy-start.4
  16.1 6.7 %shard_map.129 = bf16[4,2,1024,512]{3,2,1,0:T(8,128)(2,1)S(1)} custom-call(f32[2048,1024]{1,0:T(8,128)} %a_ref.1), custom_call_target="tpu_custom_call" | custom-call | flops 2097152 | bytes 16777216 | tf_op jit(solution)/shard_map/pallas_call | solution.py:132
  22.8 0.0 collective-permute-done.12
  22.8 61.0 %conditional.1 = ((f32[2,1024,128]{2,1,0:T(8,128)S(1)}, f32[2,1024,128]{2,1,0:T(8,128)}, f32[2,1024,128]{2,1,0:T(8,128)}, f32[2,1024,128]{2,1,0:T(8,128)})) conditional(s32[]{:T(128)} %bitcast.3, (s32[128]{0:T(128)S(1)}, f32[2,4,16,512]{3,2,1,0:T(8,128)S(1)}, f32[2,4,16,512]{3,2,1,0:T(8,128)S(1)}, ...), branch_computations={%region_0.1_spmd, %region_1.2_spmd, %region_2.3_spmd} | conditional | flops 12884901888 | bytes 75497640 | solution.py:530
  22.9 1.1 branch_1_fun.4
  24.0 17.4 %all_to_all.33.refs_1_ = f32[4,46,16,128]{3,2,1,0:T(8,128)S(1)} all-to-all(f32[4,46,16,128]{3,2,1,0:T(8,128)S(1)} %branch_1_fun.4), channel_id=1, replica_groups={{0,1,2,3},{4,5,6,7},{8,9,10,11},{12,13,14,15},{32,33,34,35},{36,37,38,3..., dimensions={0} | all-to-all | bytes 3014656 | tf_op jit(solution)/shard_map/cond/branch_1_fun/all_to_all | solution.py:93
  41.4 1.4 collective-permute-start.5
  42.8 2.3 %collective-permute-start.4 = (f32[4,46,16,128]{3,2,1,0:T(8,128)S(1)}, f32[4,46,16,128]{3,2,1,0:T(8,128)S(1)}, u32[]{:S(2)}, u32[]{:S(2)}) collective-permute-start(f32[4,46,16,128]{3,2,1,0:T(8,128)S(1)} %all_to_all.33.refs_1_), channel_id=1, source_target_pairs={{4,0},{5,1},{6,2},{7,3},{8,4},{9,5},{10,6},{11,7},{12,8},{13,9},{1... | collective-permute-start | bytes 4521992 | tf_op jit(solution)/shard_map/cond/branch_1_fun/ppermute | solution.py:84
  45.1 6.3 %branch_1_fun.5.refs_4_ = f32[8,1024,128]{2,1,0:T(8,128)S(1)} custom-call(s32[128]{0:T(128)S(1)} %get-tuple-element.31.plan_ref, bf16[4,2,1024,512]{3,2,1,0:T(8,128)(2,1)S(1)} %get-tuple-element.32.refs_0_.refs_1_, f32[4,46,16,128]{3,2,1,0:T(8,128)S(1)} %all_to_all.33.refs_1_), custom_call_target="tpu_custom_call" | custom-call | flops 3221225472 | bytes 12582912 | tf_op jit(solution)/shard_map/cond/branch_1_fun/pallas_call | solution.py:329
  51.4 11.1 %collective-permute-done.5.refs_3_ = f32[4,46,16,128]{3,2,1,0:T(8,128)S(1)} collective-permute-done((f32[4,46,16,128]{3,2,1,0:T(8,128)S(1)}, f32[4,46,16,128]{3,2,1,0:T(8,128)S(1)}, u32[]{:S(2)}, u32[]{:S(2)}) %collective-permute-start.5) | collective-permute-done | bytes 1507360 | tf_op jit(solution)/shard_map/cond/branch_1_fun/ppermute | solution.py:84
  62.5 0.0 collective-permute-done.4.refs_2_
  62.5 0.1 slice.21
  62.5 0.1 slice.20
  62.6 2.6 %collective-permute-start.6 = (f32[2,46,16,128]{3,2,1,0:T(8,128)S(1)}, f32[2,46,16,128]{3,2,1,0:T(8,128)S(1)}, u32[]{:S(2)}, u32[]{:S(2)}) collective-permute-start(f32[2,46,16,128]{3,2,1,0:T(8,128)S(1)} %slice.20), channel_id=1, source_target_pairs={{4,0},{5,1},{6,2},{7,3},{8,4},{9,5},{10,6},{11,7},{12,8},{13,9},{1... | collective-permute-start | bytes 2261000 | tf_op jit(solution)/shard_map/cond/branch_1_fun/ppermute | solution.py:84
  65.1 10.8 %branch_1_fun.6.refs_3_ = f32[8,1024,128]{2,1,0:T(8,128)S(1)} custom-call(s32[128]{0:T(128)S(1)} %get-tuple-element.31.plan_ref, bf16[4,2,1024,512]{3,2,1,0:T(8,128)(2,1)S(1)} %get-tuple-element.32.refs_0_.refs_1_, bf16[4,2,1024,512]{3,2,1,0:T(8,128)(2,1)S(1)} %get-tuple-element.32.refs_0_.refs_1_, f32[4,46,16,128]{3,2,1,0:T(8,128)S(1)} %collective-permute-done.4.refs_2_, ...), custom_call_target="tpu_custom_call" | custom-call | flops 6442450944 | bytes 12582912 | tf_op jit(solution)/shard_map/cond/branch_1_fun/pallas_call | solution.py:329
  76.0 1.2 collective-permute-done.7.refs_2_
  77.1 6.7 %branch_1_fun.7 = (f32[2,1024,128]{2,1,0:T(8,128)S(1)}, f32[2,1024,128]{2,1,0:T(8,128)}, f32[2,1024,128]{2,1,0:T(8,128)}, f32[2,1024,128]{2,1,0:T(8,128)}) custom-call(s32[128]{0:T(128)S(1)} %get-tuple-element.31.plan_ref, bf16[4,2,1024,512]{3,2,1,0:T(8,128)(2,1)S(1)} %get-tuple-element.32.refs_0_.refs_1_, ...), custom_call_target="tpu_custom_call" | custom-call | flops 3221225472 | bytes 12582912 | tf_op jit(solution)/shard_map/cond/branch_1_fun/pallas_call | solution.py:329
  83.8 3.6 %collective-permute-start.15 = (f32[2,1024,128]{2,1,0:T(8,128)}, f32[2,1024,128]{2,1,0:T(8,128)S(1)}, u32[]{:S(2)}, u32[]{:S(2)}) collective-permute-start(f32[2,1024,128]{2,1,0:T(8,128)} %get-tuple-element.92), channel_id=1, source_target_pairs={{16,0},{17,1},{18,2},{19,3},{20,4},{21,5},{22,6},{23,7},{24,8},{25... | collective-permute-start | bytes 3145736 | tf_op jit(solution)/shard_map/ppermute | solution.py:89
  87.4 0.1 collective-permute-start.14
  87.5 2.4 %collective-permute-done.15 = f32[2,1024,128]{2,1,0:T(8,128)S(1)} collective-permute-done((f32[2,1024,128]{2,1,0:T(8,128)}, f32[2,1024,128]{2,1,0:T(8,128)S(1)}, u32[]{:S(2)}, u32[]{:S(2)}) %collective-permute-start.15) | collective-permute-done | bytes 1048608 | tf_op jit(solution)/shard_map/ppermute | solution.py:89
  89.9 1.3 add.19
  91.2 2.3 %collective-permute-start.16 = (f32[2,1024,128]{2,1,0:T(8,128)S(1)}, f32[2,1024,128]{2,1,0:T(8,128)S(1)}, u32[]{:S(2)}, u32[]{:S(2)}) collective-permute-start(f32[2,1024,128]{2,1,0:T(8,128)S(1)} %add.19), channel_id=1, source_target_pairs={{32,0},{33,1},{34,2},{35,3},{36,4},{37,5},{38,6},{39,7},{40,8},{41... | collective-permute-start | bytes 3145736 | tf_op jit(solution)/shard_map/ppermute | solution.py:72
  93.6 3.3 %shard_map.131 = (bf16[640,1024]{1,0:T(8,128)(2,1)S(1)}, bf16[640,1024]{1,0:T(8,128)(2,1)S(1)}) custom-call(s32[128]{0:T(128)S(1)} %shard_map.128.plan_ref, f32[1024,512]{1,0:T(8,128)S(1)} %copy-done, f32[1024,512]{1,0:T(8,128)} %child_ref.2), custom_call_target="tpu_custom_call" | custom-call | flops 1048576 | bytes 8388608 | tf_op jit(solution)/shard_map/pallas_call | solution.py:387
  96.9 0.1 add.18
  97.0 9.2 %collective-permute-done.16 = f32[2,1024,128]{2,1,0:T(8,128)S(1)} collective-permute-done((f32[2,1024,128]{2,1,0:T(8,128)S(1)}, f32[2,1024,128]{2,1,0:T(8,128)S(1)}, u32[]{:S(2)}, u32[]{:S(2)}) %collective-permute-start.16) | collective-permute-done | bytes 1048608 | tf_op jit(solution)/shard_map/ppermute | solution.py:72
  106.2 0.1 add.20
  106.3 0.1 slice_bitcast_fusion
  106.4 1.0 collective-permute-start.17
  107.4 7.4 %collective-permute-done.17.passed_ref = f32[1024,128]{1,0:T(8,128)S(1)} collective-permute-done((f32[1024,128]{1,0:T(8,128)S(1)}, f32[1024,128]{1,0:T(8,128)S(1)}, u32[]{:S(2)}, u32[]{:S(2)}) %collective-permute-start.17) | collective-permute-done | bytes 524320 | tf_op jit(solution)/shard_map/ppermute | solution.py:72
  114.8 1.2 shard_map.132
  116.0 1.0 collective-permute-start.18
  117.0 8.2 %all_to_all.35 = f32[4,160,128]{2,1,0:T(8,128)S(1)} all-to-all(f32[4,160,128]{2,1,0:T(8,128)S(1)} %bitcast.16), channel_id=1, replica_groups={{0,1,2,3},{4,5,6,7},{8,9,10,11},{12,13,14,15},{32,33,34,35},{36,37,38,3..., dimensions={0} | all-to-all | bytes 655360 | tf_op jit(solution)/shard_map/all_to_all | solution.py:93
  125.2 0.1 pad_maximum_fusion.own_a
  125.3 5.2 %collective-permute-start.20 = (f32[2,1024,128]{2,1,0:T(8,128)S(1)}, f32[2,1024,128]{2,1,0:T(8,128)S(1)}, u32[]{:S(2)}, u32[]{:S(2)}) collective-permute-start(f32[2,1024,128]{2,1,0:T(8,128)S(1)} %pad_maximum_fusion.own_a), channel_id=1, source_target_pairs={{16,0},{17,1},{18,2},{19,3},{20,4},{21,5},{22,6},{23,7},{24,8},{25... | collective-permute-start | bytes 3145736 | tf_op jit(solution)/shard_map/ppermute | solution.py:89
  130.5 0.7 collective-permute-start.19
  131.2 8.4 %all_to_all.36 = f32[4,160,128]{2,1,0:T(8,128)S(1)} all-to-all(f32[4,160,128]{2,1,0:T(8,128)S(1)} %broadcast_in_dim.6), channel_id=1, replica_groups={{0,4,8,12},{1,5,9,13},{2,6,10,14},{3,7,11,15},{32,36,40,44},{33,37,41,4..., dimensions={0} | all-to-all | bytes 655360 | tf_op jit(solution)/shard_map/all_to_all | solution.py:93
  139.7 9.0 %all_to_all.37 = f32[4,160,128]{2,1,0:T(8,128)S(1)} all-to-all(f32[4,160,128]{2,1,0:T(8,128)S(1)} %broadcast_in_dim.7), channel_id=1, replica_groups={{0,32,64,96},{1,33,65,97},{2,34,66,98},{3,35,67,99},{4,36,68,100},{5,37..., dimensions={0} | all-to-all | bytes 655360 | tf_op jit(solution)/shard_map/all_to_all | solution.py:93
  148.7 2.3 %collective-permute-start.21 = (f32[2,1024,128]{2,1,0:T(8,128)S(1)}, f32[2,1024,128]{2,1,0:T(8,128)S(1)}, u32[]{:S(2)}, u32[]{:S(2)}) collective-permute-start(f32[2,1024,128]{2,1,0:T(8,128)S(1)} %collective-permute-done.19.own_b), channel_id=1, source_target_pairs={{16,0},{17,1},{18,2},{19,3},{20,4},{21,5},{22,6},{23,7},{24,8},{25... | collective-permute-start | bytes 3145736 | tf_op jit(solution)/shard_map/ppermute | solution.py:89
  151.0 0.1 broadcast_in_dim.8
  151.1 13.8 %all_to_all.38.own_ref = f32[4,4,160,128]{3,2,1,0:T(8,128)S(1)} all-to-all(f32[4,4,160,128]{3,2,1,0:T(8,128)S(1)} %broadcast_in_dim.8), channel_id=1, replica_groups={{0,1,2,3},{4,5,6,7},{8,9,10,11},{12,13,14,15},{32,33,34,35},{36,37,38,3..., dimensions={0} | all-to-all | bytes 2621440 | tf_op jit(solution)/shard_map/all_to_all | solution.py:93
  164.9 1.2 collective-permute-start.22
  166.1 4.9 %shard_map.133 = (f32[1024,512]{1,0:T(8,128)}, f32[1024,512]{1,0:T(8,128)}) custom-call(s32[128]{0:T(128)S(1)} %copy-done.5, f32[2,1024,128]{2,1,0:T(8,128)S(1)} %pad_maximum_fusion.own_a, f32[2,1024,128]{2,1,0:T(8,128)S(1)} %collective-permute-done.19.own_b, f32[2,1024,128]{2,1,0:T(8,128)S(1)} %collective-permute-done.20.other_a, ...), custom_call_target="tpu_custom_call" | custom-call | flops 1610612736 | bytes 8388608 | tf_op jit(solution)/shard_map/pallas_call | solution.py:456
  171.0 4.5 %shard_map.134 = (f32[512,512]{1,0:T(8,128)}, f32[512,512]{1,0:T(8,128)}, f32[512,512]{1,0:T(8,128)}) custom-call(s32[128]{0:T(128)S(1)} %copy-done.5, f32[4,4,160,128]{3,2,1,0:T(8,128)S(1)} %all_to_all.38.own_ref, f32[4,4,160,128]{3,2,1,0:T(8,128)S(1)} %collective-permute-done.22.other_ref, f32[512,512]{1,0:T(8,128)S(1)} %copy-done.1, ...), custom_call_target="tpu_custom_call" | custom-call | flops 2415919104 | bytes 10485760 | tf_op jit(solution)/shard_map/pallas_call | solution.py:503
  (24 shorter events, 0.1 us)
Async XLA Ops:
  4.4 18.4 %collective-permute-start.12 = (f32[2,4,16,512]{3,2,1,0:T(8,128)}, f32[2,4,16,512]{3,2,1,0:T(8,128)S(1)}, u32[]{:S(2)}, u32[]{:S(2)}) collective-permute-start(f32[2,4,16,512]{3,2,1,0:T(8,128)} %get-tuple-element.83), channel_id=1, source_target_pairs={{0,0},{16,1},{1,2},{17,3},{32,4},{48,5},{33,6},{49,7},{64,8},{80,9... | collective-permute-start | bytes 786440 | tf_op jit(solution)/shard_map/ppermute | solution.py:527
  8.9 13.9 %collective-permute-start.13 = (f32[2,4,16,512]{3,2,1,0:T(8,128)}, f32[2,4,16,512]{3,2,1,0:T(8,128)S(1)}, u32[]{:S(2)}, u32[]{:S(2)}) collective-permute-start(f32[2,4,16,512]{3,2,1,0:T(8,128)} %get-tuple-element.84), channel_id=1, source_target_pairs={{1,0},{17,1},{0,2},{16,3},{33,4},{49,5},{32,6},{48,7},{65,8},{81,9... | collective-permute-start | bytes 786440 | tf_op jit(solution)/shard_map/ppermute | solution.py:527
  16.0 77.5 %copy-start.4 = (s32[128]{0:T(128)}, s32[128]{0:T(128)S(1)}, u32[]{:S(2)}) copy-start(s32[128]{0:T(128)S(1)} %shard_map.128.plan_ref) | copy-start | bytes 1540
  41.4 21.1 %collective-permute-start.5 = (f32[4,46,16,128]{3,2,1,0:T(8,128)S(1)}, f32[4,46,16,128]{3,2,1,0:T(8,128)S(1)}, u32[]{:S(2)}, u32[]{:S(2)}) collective-permute-start(f32[4,46,16,128]{3,2,1,0:T(8,128)S(1)} %all_to_all.33.refs_1_), channel_id=1, source_target_pairs={{12,0},{13,1},{14,2},{15,3},{0,4},{1,5},{2,6},{3,7},{4,8},{5,9},{6... | collective-permute-start | bytes 4521992 | tf_op jit(solution)/shard_map/cond/branch_1_fun/ppermute | solution.py:84
  42.8 19.7 %collective-permute-start.4 = (f32[4,46,16,128]{3,2,1,0:T(8,128)S(1)}, f32[4,46,16,128]{3,2,1,0:T(8,128)S(1)}, u32[]{:S(2)}, u32[]{:S(2)}) collective-permute-start(f32[4,46,16,128]{3,2,1,0:T(8,128)S(1)} %all_to_all.33.refs_1_), channel_id=1, source_target_pairs={{4,0},{5,1},{6,2},{7,3},{8,4},{9,5},{10,6},{11,7},{12,8},{13,9},{1... | collective-permute-start | bytes 4521992 | tf_op jit(solution)/shard_map/cond/branch_1_fun/ppermute | solution.py:84
  62.6 13.4 %collective-permute-start.6 = (f32[2,46,16,128]{3,2,1,0:T(8,128)S(1)}, f32[2,46,16,128]{3,2,1,0:T(8,128)S(1)}, u32[]{:S(2)}, u32[]{:S(2)}) collective-permute-start(f32[2,46,16,128]{3,2,1,0:T(8,128)S(1)} %slice.20), channel_id=1, source_target_pairs={{4,0},{5,1},{6,2},{7,3},{8,4},{9,5},{10,6},{11,7},{12,8},{13,9},{1... | collective-permute-start | bytes 2261000 | tf_op jit(solution)/shard_map/cond/branch_1_fun/ppermute | solution.py:84
  65.1 12.0 %collective-permute-start.7 = (f32[2,46,16,128]{3,2,1,0:T(8,128)S(1)}, f32[2,46,16,128]{3,2,1,0:T(8,128)S(1)}, u32[]{:S(2)}, u32[]{:S(2)}) collective-permute-start(f32[2,46,16,128]{3,2,1,0:T(8,128)S(1)} %slice.21), channel_id=1, source_target_pairs={{12,0},{13,1},{14,2},{15,3},{0,4},{1,5},{2,6},{3,7},{4,8},{5,9},{6... | collective-permute-start | bytes 2261000 | tf_op jit(solution)/shard_map/cond/branch_1_fun/ppermute | solution.py:84
  83.8 9.8 %copy-start = (f32[1024,512]{1,0:T(8,128)S(1)}, f32[1024,512]{1,0:T(8,128)}, u32[]{:S(2)}) copy-start(f32[1024,512]{1,0:T(8,128)} %parent_ref.2) | copy-start | bytes 6291460
  83.8 6.1 %collective-permute-start.15 = (f32[2,1024,128]{2,1,0:T(8,128)}, f32[2,1024,128]{2,1,0:T(8,128)S(1)}, u32[]{:S(2)}, u32[]{:S(2)}) collective-permute-start(f32[2,1024,128]{2,1,0:T(8,128)} %get-tuple-element.92), channel_id=1, source_target_pairs={{16,0},{17,1},{18,2},{19,3},{20,4},{21,5},{22,6},{23,7},{24,8},{25... | collective-permute-start | bytes 3145736 | tf_op jit(solution)/shard_map/ppermute | solution.py:89
  87.4 9.4 %collective-permute-start.14 = (f32[2,1024,128]{2,1,0:T(8,128)}, f32[2,1024,128]{2,1,0:T(8,128)S(1)}, u32[]{:S(2)}, u32[]{:S(2)}) collective-permute-start(f32[2,1024,128]{2,1,0:T(8,128)} %get-tuple-element.90), channel_id=1, source_target_pairs={{16,0},{17,1},{18,2},{19,3},{20,4},{21,5},{22,6},{23,7},{24,8},{25... | collective-permute-start | bytes 3145736 | tf_op jit(solution)/shard_map/ppermute | solution.py:89
  91.2 14.9 %collective-permute-start.16 = (f32[2,1024,128]{2,1,0:T(8,128)S(1)}, f32[2,1024,128]{2,1,0:T(8,128)S(1)}, u32[]{:S(2)}, u32[]{:S(2)}) collective-permute-start(f32[2,1024,128]{2,1,0:T(8,128)S(1)} %add.19), channel_id=1, source_target_pairs={{32,0},{33,1},{34,2},{35,3},{36,4},{37,5},{38,6},{39,7},{40,8},{41... | collective-permute-start | bytes 3145736 | tf_op jit(solution)/shard_map/ppermute | solution.py:72
  106.4 8.4 %collective-permute-start.17 = (f32[1024,128]{1,0:T(8,128)S(1)}, f32[1024,128]{1,0:T(8,128)S(1)}, u32[]{:S(2)}, u32[]{:S(2)}) collective-permute-start(f32[1024,128]{1,0:T(8,128)S(1)} %get-tuple-element.116), channel_id=1, source_target_pairs={{96,0},{97,1},{98,2},{99,3},{100,4},{101,5},{102,6},{103,7},{104,8... | collective-permute-start | bytes 1572872 | tf_op jit(solution)/shard_map/ppermute | solution.py:72
  116.0 9.3 %collective-permute-start.18 = (f32[1024,128]{1,0:T(8,128)S(1)}, f32[1024,128]{1,0:T(8,128)S(1)}, u32[]{:S(2)}, u32[]{:S(2)}) collective-permute-start(f32[1024,128]{1,0:T(8,128)S(1)} %get-tuple-element.99), channel_id=1, source_target_pairs={{96,0},{97,1},{98,2},{99,3},{100,4},{101,5},{102,6},{103,7},{104,8... | collective-permute-start | bytes 1572872 | tf_op jit(solution)/shard_map/ppermute | solution.py:72
  125.3 23.4 %collective-permute-start.20 = (f32[2,1024,128]{2,1,0:T(8,128)S(1)}, f32[2,1024,128]{2,1,0:T(8,128)S(1)}, u32[]{:S(2)}, u32[]{:S(2)}) collective-permute-start(f32[2,1024,128]{2,1,0:T(8,128)S(1)} %pad_maximum_fusion.own_a), channel_id=1, source_target_pairs={{16,0},{17,1},{18,2},{19,3},{20,4},{21,5},{22,6},{23,7},{24,8},{25... | collective-permute-start | bytes 3145736 | tf_op jit(solution)/shard_map/ppermute | solution.py:89
  130.5 18.2 %collective-permute-start.19 = (f32[2,1024,128]{2,1,0:T(8,128)S(1)}, f32[2,1024,128]{2,1,0:T(8,128)S(1)}, u32[]{:S(2)}, u32[]{:S(2)}) collective-permute-start(f32[2,1024,128]{2,1,0:T(8,128)S(1)} %pad_maximum_fusion.own_a), channel_id=1, source_target_pairs={{32,0},{33,1},{34,2},{35,3},{36,4},{37,5},{38,6},{39,7},{40,8},{41... | collective-permute-start | bytes 3145736 | tf_op jit(solution)/shard_map/ppermute | solution.py:72
  148.7 17.4 %copy-start.1 = (f32[512,512]{1,0:T(8,128)S(1)}, f32[512,512]{1,0:T(8,128)}, u32[]{:S(2)}) copy-start(f32[512,512]{1,0:T(8,128)} %cross_ref.3) | copy-start | bytes 3145732
  148.7 17.4 %copy-start.5 = (s32[128]{0:T(128)S(1)}, s32[128]{0:T(128)}, u32[]{:S(2)}) copy-start(s32[128]{0:T(128)} %copy-done.4) | copy-start | bytes 1540
  148.7 16.2 %collective-permute-start.21 = (f32[2,1024,128]{2,1,0:T(8,128)S(1)}, f32[2,1024,128]{2,1,0:T(8,128)S(1)}, u32[]{:S(2)}, u32[]{:S(2)}) collective-permute-start(f32[2,1024,128]{2,1,0:T(8,128)S(1)} %collective-permute-done.19.own_b), channel_id=1, source_target_pairs={{16,0},{17,1},{18,2},{19,3},{20,4},{21,5},{22,6},{23,7},{24,8},{25... | collective-permute-start | bytes 3145736 | tf_op jit(solution)/shard_map/ppermute | solution.py:89
  164.9 6.1 %copy-start.2 = (f32[512,512]{1,0:T(8,128)S(1)}, f32[512,512]{1,0:T(8,128)}, u32[]{:S(2)}) copy-start(f32[512,512]{1,0:T(8,128)} %parent_ref.3) | copy-start | bytes 3145732
  164.9 6.1 %copy-start.3 = (f32[512,512]{1,0:T(8,128)S(1)}, f32[512,512]{1,0:T(8,128)}, u32[]{:S(2)}) copy-start(f32[512,512]{1,0:T(8,128)} %child_ref.3) | copy-start | bytes 3145732
  164.9 6.1 %collective-permute-start.22 = (f32[4,4,160,128]{3,2,1,0:T(8,128)S(1)}, f32[4,4,160,128]{3,2,1,0:T(8,128)S(1)}, u32[]{:S(2)}, u32[]{:S(2)}) collective-permute-start(f32[4,4,160,128]{3,2,1,0:T(8,128)S(1)} %all_to_all.38.own_ref), channel_id=1, source_target_pairs={{16,0},{17,1},{18,2},{19,3},{20,4},{21,5},{22,6},{23,7},{24,8},{25... | collective-permute-start | bytes 3932168 | tf_op jit(solution)/shard_map/ppermute | solution.py:89
where the time goes:
time: 176 us
  blocking collectives  56.9 us (32%)
  Pallas kernels  51 us (29%)
  starting transfers between devices  32.3 us (18%)
  waiting for transfers between devices  31.3 us (18%)
    all_to_all x5, blocking collectives, exchange(): lax.all_to_all(value, AXES, 0, 0, axis_index_groups=groups, tiled=True)  56.9 us
    pallas_call x3, Pallas kernels, product(): pl.pallas_call(kernel, grid_spec=pltpu.PrefetchScalarGridSpec(num_scalar_...  23.8 us
    ppermute x4, waiting for transfers between devices, swap_planes(): return lax.ppermute(value, AXES, pairs)  16.6 us
    ppermute x5, starting transfers between devices, swap_cores(): return lax.ppermute(value, AXES, pairs)  12.3 us
    ppermute x4, waiting for transfers between devices, fetch_far(): return lax.ppermute(value, AXES, pairs)  12.2 us
    ppermute x2, starting transfers between devices, per_device(): lax.ppermute(value, AXES, pairs)  8.74 us
    pallas_call x1, Pallas kernels, split_transposed(): pl.pallas_call(split_transposed_kernel, grid=(rows // (2 * BLK),), in_spe...  6.72 us
    ppermute x4, starting transfers between devices, fetch_far(): return lax.ppermute(value, AXES, pairs)  6.24 us
  transfers between devices with their start and end apart: 15, of which 5 were waited for; matrix products, arithmetic and copies ran while one was open for 1% of the time, Pallas kernels for 20%

commit v1 on v0

--- a/solution.py
+++ b/solution.py
@@ -122,19 +122,20 @@
     def _(o):
         parts = [a_ref[pl.ds(pl.multiple_of(BLK * i + GROUP * o, GROUP), GROUP), :] for i in range(2)]
         high, low = split(jnp.concatenate(parts, axis=0))
-        out_ref[o, 0] = high.T
-        out_ref[o, 1] = low.T
+        out_ref[0, o, 0] = high.T
+        out_ref[0, o, 1] = low.T
 
 
 def split_transposed(a):
     rows, cols = a.shape
-    out = pl.BlockSpec((SIDE, 2, cols, 2 * GROUP), lambda i: (0, 0, 0, i))
+    steps = rows // (2 * BLK)
+    out = pl.BlockSpec((1, SIDE, 2, cols, 2 * GROUP), lambda i: (i, 0, 0, 0, 0))
     return pl.pallas_call(
         split_transposed_kernel,
-        grid=(rows // (2 * BLK),),
+        grid=(steps,),
         in_specs=[pl.BlockSpec((2 * BLK, cols), lambda i: (i, 0))],
         out_specs=out,
-        out_shape=jax.ShapeDtypeStruct((SIDE, 2, cols, rows // SIDE), jnp.bfloat16),
+        out_shape=jax.ShapeDtypeStruct((steps, SIDE, 2, cols, 2 * GROUP), jnp.bfloat16),
         compiler_params=pltpu.CompilerParams(vmem_limit_bytes=50 * MIB),
         cost_estimate=pl.CostEstimate(flops=rows * cols, bytes_accessed=8 * rows * cols, transcendentals=0),
     )(a)
@@ -267,7 +268,8 @@
     tiles, refs = refs[:count], refs[count:]
     pieces, refs = refs[: sum(sizes)], refs[sum(sizes) :]
     out_refs, (panel_high, panel_low) = refs[has_earlier:-2], refs[-2:]
-    tile, depth = tiles[0].shape[2:]
+    steps, _, _, tile, lanes = tiles[0].shape
+    depth = steps * lanes
 
     @pl.when(pl.program_id(0) == 0)
     def _():
@@ -295,10 +297,10 @@
         total = None
         for g in range(count):
             rows = pl.ds(depth * g, depth)
-            both = tiles[g][0].reshape(2 * tile, depth)
+            both = jnp.concatenate([tiles[g][n, 0].reshape(2 * tile, lanes) for n in range(steps)], axis=1)
             part = jnp.dot(both, panel_high[rows, cols], preferred_element_type=jnp.float32)
             part = part[:tile] + part[tile:]
-            part += jnp.dot(tiles[g][0, 0], panel_low[rows, cols], preferred_element_type=jnp.float32)
+            part += jnp.dot(both[:tile], panel_low[rows, cols], preferred_element_type=jnp.float32)
             total = part if total is None else total + part
         return [total[:, LANES * q : LANES * (q + 1)] for q in SPAN]
 
@@ -315,14 +317,15 @@
 
 
 def product(plan, split_tile, shifts, groups, earlier=None, is_last=False):
-    _, _, cols, depth = split_tile.shape
+    steps, _, _, cols, lanes = split_tile.shape
+    depth = steps * lanes
     tile = 256
     pieces = [piece for group in groups for piece in group]
     whole = pl.BlockSpec((CHUNKS, tile, LANES), lambda i, plan: (0, i, 0))
     pair = pl.BlockSpec((2, tile, LANES), lambda i, plan: (0, i, 0))
     tiles = [
         pl.BlockSpec(
-            (1, 2, tile, depth), lambda i, plan, shift=shift: (lax.rem(plan[OUTER] + shift, SIDE), 0, i, 0))
+            (steps, 1, 2, tile, lanes), lambda i, plan, shift=shift: (0, lax.rem(plan[OUTER] + shift, SIDE), 0, i, 0))
         for shift in shifts
     ]
     kernel = functools.partial(product_kernel, [len(group) for group in groups], earlier is not None)

time: 176 us -> 172 us (0.977); the launches traced: 176 us -> 169 us
  waiting for transfers between devices: 31.3 us -> 26.6 us
    ppermute x4, waiting for transfers between devices: 12.2 us -> 7.56 us  [fetch_far(): return lax.ppermute(value, AXES, pairs)]
  transfers between devices with their start and end apart: 15 -> 15, of which waited for: 5 -> 4; matrix products, arithmetic and copies ran while one was open for 1% -> 1% of each run, Pallas kernels for 20% -> 20%
where the time goes in v1:
time: 172 us; the launch traced here: 169 us
  blocking collectives  57 us (33%)
  Pallas kernels  50 us (29%)
  starting transfers between devices  31.3 us (18%)
  waiting for transfers between devices  26.6 us (15%)
    all_to_all x5, blocking collectives, exchange(): lax.all_to_all(value, AXES, 0, 0, axis_index_groups=groups, tiled=True)  57 us
    pallas_call x3, Pallas kernels, product(): pl.pallas_call(kernel, grid_spec=pltpu.PrefetchScalarGridSpec(num_scalar_...  23.8 us
    ppermute x4, waiting for transfers between devices, swap_planes(): return lax.ppermute(value, AXES, pairs)  16.6 us
    ppermute x5, starting transfers between devices, swap_cores(): return lax.ppermute(value, AXES, pairs)  11.6 us
    ppermute x2, starting transfers between devices, per_device(): lax.ppermute(value, AXES, pairs)  8.74 us
    ppermute x4, waiting for transfers between devices, fetch_far(): return lax.ppermute(value, AXES, pairs)  7.56 us
    ppermute x4, starting transfers between devices, fetch_far(): return lax.ppermute(value, AXES, pairs)  5.89 us
    pallas_call x1, Pallas kernels, split_transposed(): pl.pallas_call(split_transposed_kernel, grid=(steps,), in_specs=[pl.Block...  5.67 us
  transfers between devices with their start and end apart: 15, of which 4 were waited for; matrix products, arithmetic and copies ran while one was open for 1% of the time, Pallas kernels for 20%

profile of v1, /device:TPU:1, one launch (start us, length us, event | category | flops | bytes accessed | tf_op | source)
XLA Modules:
  0.0 168.9 jit_solution(14420840764147952725)
XLA Ops:
  0.6 1.2 dynamic-slice_bitcast_fusion.place_ref
  1.8 2.6 %shard_map.130 = (f32[2,4,16,512]{3,2,1,0:T(8,128)}, f32[2,4,16,512]{3,2,1,0:T(8,128)}) custom-call(s32[5]{0:T(128)} %dynamic-slice_bitcast_fusion.place_ref, f32[4,256,512]{2,1,0:T(8,128)} %bitcast.13, f32[4,256,512]{2,1,0:T(8,128)} %bitcast.14, f32[4,256,512]{2,1,0:T(8,128)} %bitcast.17, f32[4,256,512]{2,1,0:T(8,128)} %bitcast.18), custom_call_target="tpu_custom_call" | custom-call | bytes 1048576 | tf_op jit(solution)/shard_map/pallas_call | solution.py:221
  4.4 4.5 %collective-permute-start.12 = (f32[2,4,16,512]{3,2,1,0:T(8,128)}, f32[2,4,16,512]{3,2,1,0:T(8,128)S(1)}, u32[]{:S(2)}, u32[]{:S(2)}) collective-permute-start(f32[2,4,16,512]{3,2,1,0:T(8,128)} %get-tuple-element.83), channel_id=1, source_target_pairs={{0,0},{16,1},{1,2},{17,3},{32,4},{48,5},{33,6},{49,7},{64,8},{80,9... | collective-permute-start | bytes 786440 | tf_op jit(solution)/shard_map/ppermute | solution.py:530
  8.9 4.2 %collective-permute-start.13 = (f32[2,4,16,512]{3,2,1,0:T(8,128)}, f32[2,4,16,512]{3,2,1,0:T(8,128)S(1)}, u32[]{:S(2)}, u32[]{:S(2)}) collective-permute-start(f32[2,4,16,512]{3,2,1,0:T(8,128)} %get-tuple-element.84), channel_id=1, source_target_pairs={{1,0},{17,1},{0,2},{16,3},{33,4},{49,5},{32,6},{48,7},{65,8},{81,9... | collective-permute-start | bytes 786440 | tf_op jit(solution)/shard_map/ppermute | solution.py:530
  13.2 2.9 %shard_map.128.plan_ref = s32[128]{0:T(128)S(1)} custom-call(s32[5]{0:T(128)} %dynamic-slice_bitcast_fusion.place_ref, s32[2,64]{1,0:T(2,128)} %structure_ref.1, s32[2]{0:T(128)} %widths_ref.1), custom_call_target="tpu_custom_call" | custom-call | tf_op jit(solution)/shard_map/pallas_call | solution.py:202
  16.0 0.0 copy-start.4
  16.1 5.7 %shard_map.129 = bf16[4,4,2,1024,128]{4,3,2,1,0:T(8,128)(2,1)S(1)} custom-call(f32[2048,1024]{1,0:T(8,128)} %a_ref.1), custom_call_target="tpu_custom_call" | custom-call | flops 2097152 | bytes 16777216 | tf_op jit(solution)/shard_map/pallas_call | solution.py:133
  21.7 0.0 collective-permute-done.13
  21.8 54.6 %conditional.1 = ((f32[2,1024,128]{2,1,0:T(8,128)S(1)}, f32[2,1024,128]{2,1,0:T(8,128)}, f32[2,1024,128]{2,1,0:T(8,128)}, f32[2,1024,128]{2,1,0:T(8,128)})) conditional(s32[]{:T(128)} %bitcast.3, (s32[128]{0:T(128)S(1)}, f32[2,4,16,512]{3,2,1,0:T(8,128)S(1)}, f32[2,4,16,512]{3,2,1,0:T(8,128)S(1)}, ...), branch_computations={%region_0.1_spmd, %region_1.2_spmd, %region_2.3_spmd} | conditional | flops 12884901888 | bytes 75497640 | solution.py:533
  21.8 1.1 branch_0_fun.4
  22.9 16.0 %all_to_all.32.refs_1_ = f32[4,36,16,128]{3,2,1,0:T(8,128)S(1)} all-to-all(f32[4,36,16,128]{3,2,1,0:T(8,128)S(1)} %branch_0_fun.4), channel_id=1, replica_groups={{0,1,2,3},{4,5,6,7},{8,9,10,11},{12,13,14,15},{32,33,34,35},{36,37,38,3..., dimensions={0} | all-to-all | bytes 2359296 | tf_op jit(solution)/shard_map/cond/branch_0_fun/all_to_all | solution.py:93
  38.9 1.4 collective-permute-start.1
  40.4 1.9 %collective-permute-start = (f32[4,36,16,128]{3,2,1,0:T(8,128)S(1)}, f32[4,36,16,128]{3,2,1,0:T(8,128)S(1)}, u32[]{:S(2)}, u32[]{:S(2)}) collective-permute-start(f32[4,36,16,128]{3,2,1,0:T(8,128)S(1)} %all_to_all.32.refs_1_), channel_id=1, source_target_pairs={{4,0},{5,1},{6,2},{7,3},{8,4},{9,5},{10,6},{11,7},{12,8},{13,9},{1... | collective-permute-start | bytes 3538952 | tf_op jit(solution)/shard_map/cond/branch_0_fun/ppermute | solution.py:84
  42.3 6.3 %branch_0_fun.5.refs_4_ = f32[8,1024,128]{2,1,0:T(8,128)S(1)} custom-call(s32[128]{0:T(128)S(1)} %get-tuple-element.24.plan_ref, bf16[4,4,2,1024,128]{4,3,2,1,0:T(8,128)(2,1)S(1)} %get-tuple-element.25.refs_0_.refs_1_, f32[4,36,16,128]{3,2,1,0:T(8,128)S(1)} %all_to_all.32.refs_1_), custom_call_target="tpu_custom_call" | custom-call | flops 3221225472 | bytes 12582912 | tf_op jit(solution)/shard_map/cond/branch_0_fun/pallas_call | solution.py:332
  48.6 7.6 %collective-permute-done.1.refs_3_ = f32[4,36,16,128]{3,2,1,0:T(8,128)S(1)} collective-permute-done((f32[4,36,16,128]{3,2,1,0:T(8,128)S(1)}, f32[4,36,16,128]{3,2,1,0:T(8,128)S(1)}, u32[]{:S(2)}, u32[]{:S(2)}) %collective-permute-start.1) | collective-permute-done | bytes 1179680 | tf_op jit(solution)/shard_map/cond/branch_0_fun/ppermute | solution.py:84
  56.2 2.6 %collective-permute-start.2 = (f32[2,36,16,128]{3,2,1,0:T(8,128)S(1)}, f32[2,36,16,128]{3,2,1,0:T(8,128)S(1)}, u32[]{:S(2)}, u32[]{:S(2)}) collective-permute-start(f32[2,36,16,128]{3,2,1,0:T(8,128)S(1)} %slice.18), channel_id=1, source_target_pairs={{4,0},{5,1},{6,2},{7,3},{8,4},{9,5},{10,6},{11,7},{12,8},{13,9},{1... | collective-permute-start | bytes 1769480 | tf_op jit(solution)/shard_map/cond/branch_0_fun/ppermute | solution.py:84
  58.8 10.9 %branch_0_fun.6.refs_3_ = f32[8,1024,128]{2,1,0:T(8,128)S(1)} custom-call(s32[128]{0:T(128)S(1)} %get-tuple-element.24.plan_ref, bf16[4,4,2,1024,128]{4,3,2,1,0:T(8,128)(2,1)S(1)} %get-tuple-element.25.refs_0_.refs_1_, bf16[4,4,2,1024,128]{4,3,2,1,0:T(8,128)(2,1)S(1)} %get-tuple-element.25.refs_0_.refs_1_, ...), custom_call_target="tpu_custom_call" | custom-call | flops 6442450944 | bytes 12582912 | tf_op jit(solution)/shard_map/cond/branch_0_fun/pallas_call | solution.py:332
  69.7 0.0 collective-permute-done.3.refs_2_
  69.7 6.7 %branch_0_fun.7 = (f32[2,1024,128]{2,1,0:T(8,128)S(1)}, f32[2,1024,128]{2,1,0:T(8,128)}, f32[2,1024,128]{2,1,0:T(8,128)}, f32[2,1024,128]{2,1,0:T(8,128)}) custom-call(s32[128]{0:T(128)S(1)} %get-tuple-element.24.plan_ref, bf16[4,4,2,1024,128]{4,3,2,1,0:T(8,128)(2,1)S(1)} %get-tuple-element.25.refs_0_.refs_1_, ...), custom_call_target="tpu_custom_call" | custom-call | flops 3221225472 | bytes 12582912 | tf_op jit(solution)/shard_map/cond/branch_0_fun/pallas_call | solution.py:332
  76.4 2.9 %collective-permute-start.15 = (f32[2,1024,128]{2,1,0:T(8,128)}, f32[2,1024,128]{2,1,0:T(8,128)S(1)}, u32[]{:S(2)}, u32[]{:S(2)}) collective-permute-start(f32[2,1024,128]{2,1,0:T(8,128)} %get-tuple-element.92), channel_id=1, source_target_pairs={{16,0},{17,1},{18,2},{19,3},{20,4},{21,5},{22,6},{23,7},{24,8},{25... | collective-permute-start | bytes 3145736 | tf_op jit(solution)/shard_map/ppermute | solution.py:89
  79.3 0.1 collective-permute-start.14
  79.4 2.4 %collective-permute-done.15 = f32[2,1024,128]{2,1,0:T(8,128)S(1)} collective-permute-done((f32[2,1024,128]{2,1,0:T(8,128)}, f32[2,1024,128]{2,1,0:T(8,128)S(1)}, u32[]{:S(2)}, u32[]{:S(2)}) %collective-permute-start.15) | collective-permute-done | bytes 1048608 | tf_op jit(solution)/shard_map/ppermute | solution.py:89
  81.8 1.3 add.19
  83.1 2.3 %collective-permute-start.16 = (f32[2,1024,128]{2,1,0:T(8,128)S(1)}, f32[2,1024,128]{2,1,0:T(8,128)S(1)}, u32[]{:S(2)}, u32[]{:S(2)}) collective-permute-start(f32[2,1024,128]{2,1,0:T(8,128)S(1)} %add.19), channel_id=1, source_target_pairs={{32,0},{33,1},{34,2},{35,3},{36,4},{37,5},{38,6},{39,7},{40,8},{41... | collective-permute-start | bytes 3145736 | tf_op jit(solution)/shard_map/ppermute | solution.py:72
  85.5 3.3 %shard_map.131 = (bf16[640,1024]{1,0:T(8,128)(2,1)S(1)}, bf16[640,1024]{1,0:T(8,128)(2,1)S(1)}) custom-call(s32[128]{0:T(128)S(1)} %shard_map.128.plan_ref, f32[1024,512]{1,0:T(8,128)S(1)} %copy-done, f32[1024,512]{1,0:T(8,128)} %child_ref.2), custom_call_target="tpu_custom_call" | custom-call | flops 1048576 | bytes 8388608 | tf_op jit(solution)/shard_map/pallas_call | solution.py:390
  88.8 0.0 collective-permute-done.14
  88.8 0.1 add.18
  88.9 9.2 %collective-permute-done.16 = f32[2,1024,128]{2,1,0:T(8,128)S(1)} collective-permute-done((f32[2,1024,128]{2,1,0:T(8,128)S(1)}, f32[2,1024,128]{2,1,0:T(8,128)S(1)}, u32[]{:S(2)}, u32[]{:S(2)}) %collective-permute-start.16) | collective-permute-done | bytes 1048608 | tf_op jit(solution)/shard_map/ppermute | solution.py:72
  98.1 0.1 add.20
  98.2 0.1 slice_bitcast_fusion
  98.3 1.0 collective-permute-start.17
  99.3 7.4 %collective-permute-done.17.passed_ref = f32[1024,128]{1,0:T(8,128)S(1)} collective-permute-done((f32[1024,128]{1,0:T(8,128)S(1)}, f32[1024,128]{1,0:T(8,128)S(1)}, u32[]{:S(2)}, u32[]{:S(2)}) %collective-permute-start.17) | collective-permute-done | bytes 524320 | tf_op jit(solution)/shard_map/ppermute | solution.py:72
  106.7 1.2 shard_map.132
  107.9 1.0 collective-permute-start.18
  108.9 9.7 %all_to_all.35 = f32[4,160,128]{2,1,0:T(8,128)S(1)} all-to-all(f32[4,160,128]{2,1,0:T(8,128)S(1)} %bitcast.16), channel_id=1, replica_groups={{0,1,2,3},{4,5,6,7},{8,9,10,11},{12,13,14,15},{32,33,34,35},{36,37,38,3..., dimensions={0} | all-to-all | bytes 655360 | tf_op jit(solution)/shard_map/all_to_all | solution.py:93
  118.6 0.0 collective-permute-done.18
  118.6 0.1 pad_maximum_fusion.own_a
  118.7 3.8 %collective-permute-start.20 = (f32[2,1024,128]{2,1,0:T(8,128)S(1)}, f32[2,1024,128]{2,1,0:T(8,128)S(1)}, u32[]{:S(2)}, u32[]{:S(2)}) collective-permute-start(f32[2,1024,128]{2,1,0:T(8,128)S(1)} %pad_maximum_fusion.own_a), channel_id=1, source_target_pairs={{16,0},{17,1},{18,2},{19,3},{20,4},{21,5},{22,6},{23,7},{24,8},{25... | collective-permute-start | bytes 3145736 | tf_op jit(solution)/shard_map/ppermute | solution.py:89
  122.4 0.7 collective-permute-start.19
  123.2 8.3 %all_to_all.36 = f32[4,160,128]{2,1,0:T(8,128)S(1)} all-to-all(f32[4,160,128]{2,1,0:T(8,128)S(1)} %broadcast_in_dim.6), channel_id=1, replica_groups={{0,4,8,12},{1,5,9,13},{2,6,10,14},{3,7,11,15},{32,36,40,44},{33,37,41,4..., dimensions={0} | all-to-all | bytes 655360 | tf_op jit(solution)/shard_map/all_to_all | solution.py:93
  131.5 9.2 %all_to_all.37 = f32[4,160,128]{2,1,0:T(8,128)S(1)} all-to-all(f32[4,160,128]{2,1,0:T(8,128)S(1)} %broadcast_in_dim.7), channel_id=1, replica_groups={{0,32,64,96},{1,33,65,97},{2,34,66,98},{3,35,67,99},{4,36,68,100},{5,37..., dimensions={0} | all-to-all | bytes 655360 | tf_op jit(solution)/shard_map/all_to_all | solution.py:93
  140.7 0.0 collective-permute-done.20.other_a
  140.7 3.7 %collective-permute-start.21 = (f32[2,1024,128]{2,1,0:T(8,128)S(1)}, f32[2,1024,128]{2,1,0:T(8,128)S(1)}, u32[]{:S(2)}, u32[]{:S(2)}) collective-permute-start(f32[2,1024,128]{2,1,0:T(8,128)S(1)} %collective-permute-done.19.own_b), channel_id=1, source_target_pairs={{16,0},{17,1},{18,2},{19,3},{20,4},{21,5},{22,6},{23,7},{24,8},{25... | collective-permute-start | bytes 3145736 | tf_op jit(solution)/shard_map/ppermute | solution.py:89
  144.4 0.1 broadcast_in_dim.8
  144.5 13.8 %all_to_all.38.own_ref = f32[4,4,160,128]{3,2,1,0:T(8,128)S(1)} all-to-all(f32[4,4,160,128]{3,2,1,0:T(8,128)S(1)} %broadcast_in_dim.8), channel_id=1, replica_groups={{0,1,2,3},{4,5,6,7},{8,9,10,11},{12,13,14,15},{32,33,34,35},{36,37,38,3..., dimensions={0} | all-to-all | bytes 2621440 | tf_op jit(solution)/shard_map/all_to_all | solution.py:93
  158.3 1.2 collective-permute-start.22
  159.5 4.9 %shard_map.133 = (f32[1024,512]{1,0:T(8,128)}, f32[1024,512]{1,0:T(8,128)}) custom-call(s32[128]{0:T(128)S(1)} %copy-done.5, f32[2,1024,128]{2,1,0:T(8,128)S(1)} %pad_maximum_fusion.own_a, f32[2,1024,128]{2,1,0:T(8,128)S(1)} %collective-permute-done.19.own_b, f32[2,1024,128]{2,1,0:T(8,128)S(1)} %collective-permute-done.20.other_a, ...), custom_call_target="tpu_custom_call" | custom-call | flops 1610612736 | bytes 8388608 | tf_op jit(solution)/shard_map/pallas_call | solution.py:459
  164.4 4.5 %shard_map.134 = (f32[512,512]{1,0:T(8,128)}, f32[512,512]{1,0:T(8,128)}, f32[512,512]{1,0:T(8,128)}) custom-call(s32[128]{0:T(128)S(1)} %copy-done.5, f32[4,4,160,128]{3,2,1,0:T(8,128)S(1)} %all_to_all.38.own_ref, f32[4,4,160,128]{3,2,1,0:T(8,128)S(1)} %collective-permute-done.22.other_ref, f32[512,512]{1,0:T(8,128)S(1)} %copy-done.1, ...), custom_call_target="tpu_custom_call" | custom-call | flops 2415919104 | bytes 10485760 | tf_op jit(solution)/shard_map/pallas_call | solution.py:506
  (24 shorter events, 0.2 us)
Async XLA Ops:
  4.4 17.3 %collective-permute-start.12 = (f32[2,4,16,512]{3,2,1,0:T(8,128)}, f32[2,4,16,512]{3,2,1,0:T(8,128)S(1)}, u32[]{:S(2)}, u32[]{:S(2)}) collective-permute-start(f32[2,4,16,512]{3,2,1,0:T(8,128)} %get-tuple-element.83), channel_id=1, source_target_pairs={{0,0},{16,1},{1,2},{17,3},{32,4},{48,5},{33,6},{49,7},{64,8},{80,9... | collective-permute-start | bytes 786440 | tf_op jit(solution)/shard_map/ppermute | solution.py:530
  8.9 12.8 %collective-permute-start.13 = (f32[2,4,16,512]{3,2,1,0:T(8,128)}, f32[2,4,16,512]{3,2,1,0:T(8,128)S(1)}, u32[]{:S(2)}, u32[]{:S(2)}) collective-permute-start(f32[2,4,16,512]{3,2,1,0:T(8,128)} %get-tuple-element.84), channel_id=1, source_target_pairs={{1,0},{17,1},{0,2},{16,3},{33,4},{49,5},{32,6},{48,7},{65,8},{81,9... | collective-permute-start | bytes 786440 | tf_op jit(solution)/shard_map/ppermute | solution.py:530
  16.0 69.4 %copy-start.4 = (s32[128]{0:T(128)}, s32[128]{0:T(128)S(1)}, u32[]{:S(2)}) copy-start(s32[128]{0:T(128)S(1)} %shard_map.128.plan_ref) | copy-start | bytes 1540
  38.9 17.2 %collective-permute-start.1 = (f32[4,36,16,128]{3,2,1,0:T(8,128)S(1)}, f32[4,36,16,128]{3,2,1,0:T(8,128)S(1)}, u32[]{:S(2)}, u32[]{:S(2)}) collective-permute-start(f32[4,36,16,128]{3,2,1,0:T(8,128)S(1)} %all_to_all.32.refs_1_), channel_id=1, source_target_pairs={{12,0},{13,1},{14,2},{15,3},{0,4},{1,5},{2,6},{3,7},{4,8},{5,9},{6... | collective-permute-start | bytes 3538952 | tf_op jit(solution)/shard_map/cond/branch_0_fun/ppermute | solution.py:84
  40.4 15.8 %collective-permute-start = (f32[4,36,16,128]{3,2,1,0:T(8,128)S(1)}, f32[4,36,16,128]{3,2,1,0:T(8,128)S(1)}, u32[]{:S(2)}, u32[]{:S(2)}) collective-permute-start(f32[4,36,16,128]{3,2,1,0:T(8,128)S(1)} %all_to_all.32.refs_1_), channel_id=1, source_target_pairs={{4,0},{5,1},{6,2},{7,3},{8,4},{9,5},{10,6},{11,7},{12,8},{13,9},{1... | collective-permute-start | bytes 3538952 | tf_op jit(solution)/shard_map/cond/branch_0_fun/ppermute | solution.py:84
  56.2 13.4 %collective-permute-start.2 = (f32[2,36,16,128]{3,2,1,0:T(8,128)S(1)}, f32[2,36,16,128]{3,2,1,0:T(8,128)S(1)}, u32[]{:S(2)}, u32[]{:S(2)}) collective-permute-start(f32[2,36,16,128]{3,2,1,0:T(8,128)S(1)} %slice.18), channel_id=1, source_target_pairs={{4,0},{5,1},{6,2},{7,3},{8,4},{9,5},{10,6},{11,7},{12,8},{13,9},{1... | collective-permute-start | bytes 1769480 | tf_op jit(solution)/shard_map/cond/branch_0_fun/ppermute | solution.py:84
  58.8 10.9 %collective-permute-start.3 = (f32[2,36,16,128]{3,2,1,0:T(8,128)S(1)}, f32[2,36,16,128]{3,2,1,0:T(8,128)S(1)}, u32[]{:S(2)}, u32[]{:S(2)}) collective-permute-start(f32[2,36,16,128]{3,2,1,0:T(8,128)S(1)} %slice.19), channel_id=1, source_target_pairs={{12,0},{13,1},{14,2},{15,3},{0,4},{1,5},{2,6},{3,7},{4,8},{5,9},{6... | collective-permute-start | bytes 1769480 | tf_op jit(solution)/shard_map/cond/branch_0_fun/ppermute | solution.py:84
  76.4 9.1 %copy-start = (f32[1024,512]{1,0:T(8,128)S(1)}, f32[1024,512]{1,0:T(8,128)}, u32[]{:S(2)}) copy-start(f32[1024,512]{1,0:T(8,128)} %parent_ref.2) | copy-start | bytes 6291460
  76.4 5.4 %collective-permute-start.15 = (f32[2,1024,128]{2,1,0:T(8,128)}, f32[2,1024,128]{2,1,0:T(8,128)S(1)}, u32[]{:S(2)}, u32[]{:S(2)}) collective-permute-start(f32[2,1024,128]{2,1,0:T(8,128)} %get-tuple-element.92), channel_id=1, source_target_pairs={{16,0},{17,1},{18,2},{19,3},{20,4},{21,5},{22,6},{23,7},{24,8},{25... | collective-permute-start | bytes 3145736 | tf_op jit(solution)/shard_map/ppermute | solution.py:89
  79.3 9.4 %collective-permute-start.14 = (f32[2,1024,128]{2,1,0:T(8,128)}, f32[2,1024,128]{2,1,0:T(8,128)S(1)}, u32[]{:S(2)}, u32[]{:S(2)}) collective-permute-start(f32[2,1024,128]{2,1,0:T(8,128)} %get-tuple-element.90), channel_id=1, source_target_pairs={{16,0},{17,1},{18,2},{19,3},{20,4},{21,5},{22,6},{23,7},{24,8},{25... | collective-permute-start | bytes 3145736 | tf_op jit(solution)/shard_map/ppermute | solution.py:89
  83.1 14.9 %collective-permute-start.16 = (f32[2,1024,128]{2,1,0:T(8,128)S(1)}, f32[2,1024,128]{2,1,0:T(8,128)S(1)}, u32[]{:S(2)}, u32[]{:S(2)}) collective-permute-start(f32[2,1024,128]{2,1,0:T(8,128)S(1)} %add.19), channel_id=1, source_target_pairs={{32,0},{33,1},{34,2},{35,3},{36,4},{37,5},{38,6},{39,7},{40,8},{41... | collective-permute-start | bytes 3145736 | tf_op jit(solution)/shard_map/ppermute | solution.py:72
  98.3 8.4 %collective-permute-start.17 = (f32[1024,128]{1,0:T(8,128)S(1)}, f32[1024,128]{1,0:T(8,128)S(1)}, u32[]{:S(2)}, u32[]{:S(2)}) collective-permute-start(f32[1024,128]{1,0:T(8,128)S(1)} %get-tuple-element.116), channel_id=1, source_target_pairs={{96,0},{97,1},{98,2},{99,3},{100,4},{101,5},{102,6},{103,7},{104,8... | collective-permute-start | bytes 1572872 | tf_op jit(solution)/shard_map/ppermute | solution.py:72
  107.9 10.7 %collective-permute-start.18 = (f32[1024,128]{1,0:T(8,128)S(1)}, f32[1024,128]{1,0:T(8,128)S(1)}, u32[]{:S(2)}, u32[]{:S(2)}) collective-permute-start(f32[1024,128]{1,0:T(8,128)S(1)} %get-tuple-element.99), channel_id=1, source_target_pairs={{96,0},{97,1},{98,2},{99,3},{100,4},{101,5},{102,6},{103,7},{104,8... | collective-permute-start | bytes 1572872 | tf_op jit(solution)/shard_map/ppermute | solution.py:72
  118.7 22.0 %collective-permute-start.20 = (f32[2,1024,128]{2,1,0:T(8,128)S(1)}, f32[2,1024,128]{2,1,0:T(8,128)S(1)}, u32[]{:S(2)}, u32[]{:S(2)}) collective-permute-start(f32[2,1024,128]{2,1,0:T(8,128)S(1)} %pad_maximum_fusion.own_a), channel_id=1, source_target_pairs={{16,0},{17,1},{18,2},{19,3},{20,4},{21,5},{22,6},{23,7},{24,8},{25... | collective-permute-start | bytes 3145736 | tf_op jit(solution)/shard_map/ppermute | solution.py:89
  122.4 18.2 %collective-permute-start.19 = (f32[2,1024,128]{2,1,0:T(8,128)S(1)}, f32[2,1024,128]{2,1,0:T(8,128)S(1)}, u32[]{:S(2)}, u32[]{:S(2)}) collective-permute-start(f32[2,1024,128]{2,1,0:T(8,128)S(1)} %pad_maximum_fusion.own_a), channel_id=1, source_target_pairs={{32,0},{33,1},{34,2},{35,3},{36,4},{37,5},{38,6},{39,7},{40,8},{41... | collective-permute-start | bytes 3145736 | tf_op jit(solution)/shard_map/ppermute | solution.py:72
  140.7 18.8 %copy-start.1 = (f32[512,512]{1,0:T(8,128)S(1)}, f32[512,512]{1,0:T(8,128)}, u32[]{:S(2)}) copy-start(f32[512,512]{1,0:T(8,128)} %cross_ref.3) | copy-start | bytes 3145732
  140.7 18.8 %copy-start.5 = (s32[128]{0:T(128)S(1)}, s32[128]{0:T(128)}, u32[]{:S(2)}) copy-start(s32[128]{0:T(128)} %copy-done.4) | copy-start | bytes 1540
  140.7 17.6 %collective-permute-start.21 = (f32[2,1024,128]{2,1,0:T(8,128)S(1)}, f32[2,1024,128]{2,1,0:T(8,128)S(1)}, u32[]{:S(2)}, u32[]{:S(2)}) collective-permute-start(f32[2,1024,128]{2,1,0:T(8,128)S(1)} %collective-permute-done.19.own_b), channel_id=1, source_target_pairs={{16,0},{17,1},{18,2},{19,3},{20,4},{21,5},{22,6},{23,7},{24,8},{25... | collective-permute-start | bytes 3145736 | tf_op jit(solution)/shard_map/ppermute | solution.py:89
  158.3 6.1 %copy-start.2 = (f32[512,512]{1,0:T(8,128)S(1)}, f32[512,512]{1,0:T(8,128)}, u32[]{:S(2)}) copy-start(f32[512,512]{1,0:T(8,128)} %parent_ref.3) | copy-start | bytes 3145732
  158.3 6.1 %copy-start.3 = (f32[512,512]{1,0:T(8,128)S(1)}, f32[512,512]{1,0:T(8,128)}, u32[]{:S(2)}) copy-start(f32[512,512]{1,0:T(8,128)} %child_ref.3) | copy-start | bytes 3145732
  158.3 6.1 %collective-permute-start.22 = (f32[4,4,160,128]{3,2,1,0:T(8,128)S(1)}, f32[4,4,160,128]{3,2,1,0:T(8,128)S(1)}, u32[]{:S(2)}, u32[]{:S(2)}) collective-permute-start(f32[4,4,160,128]{3,2,1,0:T(8,128)S(1)} %all_to_all.38.own_ref), channel_id=1, source_target_pairs={{16,0},{17,1},{18,2},{19,3},{20,4},{21,5},{22,6},{23,7},{24,8},{25... | collective-permute-start | bytes 3932168 | tf_op jit(solution)/shard_map/ppermute | solution.py:89

commit v2 on v1

--- a/solution.py
+++ b/solution.py
@@ -148,12 +148,6 @@
 def plan_kernel(place_ref, structure_ref, widths_ref, plan_ref, counts):
     r, c = place_ref[0], place_ref[1]
     chunks = [(widths_ref[i] + LANES - 1) // LANES for i in range(2)]
-
-    def zero(i, _):
-        plan_ref[i] = 0
-        return 0
-
-    lax.fori_loop(0, PLAN_SIZE, zero, 0)
 
     def count(col, _):
         total = jnp.int32(0)

time: 172 us -> 174 us (1.012); the launches traced: 169 us -> 174 us
  waiting for transfers between devices: 26.6 us -> 32 us
    ppermute x4, waiting for transfers between devices: 7.56 us -> 12.2 us  [fetch_far(): return lax.ppermute(value, AXES, pairs)]
  transfers between devices with their start and end apart: 15 -> 15, of which waited for: 4 -> 6; matrix products, arithmetic and copies ran while one was open for 1% -> 1% of each run, Pallas kernels for 20% -> 19%
where the time goes in v2:
time: 174 us
  blocking collectives  58 us (33%)
  Pallas kernels  49.2 us (28%)
  waiting for transfers between devices  32 us (18%)
  starting transfers between devices  30.4 us (17%)
    all_to_all x5, blocking collectives, exchange(): lax.all_to_all(value, AXES, 0, 0, axis_index_groups=groups, tiled=True)  58 us
    pallas_call x3, Pallas kernels, product(): pl.pallas_call(kernel, grid_spec=pltpu.PrefetchScalarGridSpec(num_scalar_...  23.8 us
    ppermute x4, waiting for transfers between devices, swap_planes(): return lax.ppermute(value, AXES, pairs)  17.4 us
    ppermute x5, starting transfers between devices, swap_cores(): return lax.ppermute(value, AXES, pairs)  12.5 us
    ppermute x4, waiting for transfers between devices, fetch_far(): return lax.ppermute(value, AXES, pairs)  12.2 us
    ppermute x2, starting transfers between devices, per_device(): lax.ppermute(value, AXES, pairs)  8.74 us
    pallas_call x1, Pallas kernels, split_transposed(): pl.pallas_call(split_transposed_kernel, grid=(steps,), in_specs=[pl.Block...  5.67 us
    ppermute x4, starting transfers between devices, fetch_far(): return lax.ppermute(value, AXES, pairs)  5.22 us
  transfers between devices with their start and end apart: 15, of which 6 were waited for; matrix products, arithmetic and copies ran while one was open for 1% of the time, Pallas kernels for 19%

profile of v2, /device:TPU:1, one launch (start us, length us, event | category | flops | bytes accessed | tf_op | source)
XLA Modules:
  0.0 173.7 jit_solution(18079638269278790524)
XLA Ops:
  0.6 1.2 dynamic-slice_bitcast_fusion.place_ref
  1.8 2.6 %shard_map.130 = (f32[2,4,16,512]{3,2,1,0:T(8,128)}, f32[2,4,16,512]{3,2,1,0:T(8,128)}) custom-call(s32[5]{0:T(128)} %dynamic-slice_bitcast_fusion.place_ref, f32[4,256,512]{2,1,0:T(8,128)} %bitcast.13, f32[4,256,512]{2,1,0:T(8,128)} %bitcast.14, f32[4,256,512]{2,1,0:T(8,128)} %bitcast.17, f32[4,256,512]{2,1,0:T(8,128)} %bitcast.18), custom_call_target="tpu_custom_call" | custom-call | bytes 1048576 | tf_op jit(solution)/shard_map/pallas_call | solution.py:215
  4.4 4.5 %collective-permute-start.12 = (f32[2,4,16,512]{3,2,1,0:T(8,128)}, f32[2,4,16,512]{3,2,1,0:T(8,128)S(1)}, u32[]{:S(2)}, u32[]{:S(2)}) collective-permute-start(f32[2,4,16,512]{3,2,1,0:T(8,128)} %get-tuple-element.83), channel_id=1, source_target_pairs={{0,0},{16,1},{1,2},{17,3},{32,4},{48,5},{33,6},{49,7},{64,8},{80,9... | collective-permute-start | bytes 786440 | tf_op jit(solution)/shard_map/ppermute | solution.py:524
  8.9 4.2 %collective-permute-start.13 = (f32[2,4,16,512]{3,2,1,0:T(8,128)}, f32[2,4,16,512]{3,2,1,0:T(8,128)S(1)}, u32[]{:S(2)}, u32[]{:S(2)}) collective-permute-start(f32[2,4,16,512]{3,2,1,0:T(8,128)} %get-tuple-element.84), channel_id=1, source_target_pairs={{1,0},{17,1},{0,2},{16,3},{33,4},{49,5},{32,6},{48,7},{65,8},{81,9... | collective-permute-start | bytes 786440 | tf_op jit(solution)/shard_map/ppermute | solution.py:524
  13.2 2.1 %shard_map.128.plan_ref = s32[128]{0:T(128)S(1)} custom-call(s32[5]{0:T(128)} %dynamic-slice_bitcast_fusion.place_ref, s32[2,64]{1,0:T(2,128)} %structure_ref.1, s32[2]{0:T(128)} %widths_ref.1), custom_call_target="tpu_custom_call" | custom-call | tf_op jit(solution)/shard_map/pallas_call | solution.py:196
  15.2 0.0 copy-start.4
  15.2 5.7 %shard_map.129 = bf16[4,4,2,1024,128]{4,3,2,1,0:T(8,128)(2,1)S(1)} custom-call(f32[2048,1024]{1,0:T(8,128)} %a_ref.1), custom_call_target="tpu_custom_call" | custom-call | flops 2097152 | bytes 16777216 | tf_op jit(solution)/shard_map/pallas_call | solution.py:133
  20.9 0.0 collective-permute-done.12
  21.0 61.3 %conditional.1 = ((f32[2,1024,128]{2,1,0:T(8,128)S(1)}, f32[2,1024,128]{2,1,0:T(8,128)}, f32[2,1024,128]{2,1,0:T(8,128)}, f32[2,1024,128]{2,1,0:T(8,128)})) conditional(s32[]{:T(128)} %bitcast.3, (s32[128]{0:T(128)S(1)}, f32[2,4,16,512]{3,2,1,0:T(8,128)S(1)}, f32[2,4,16,512]{3,2,1,0:T(8,128)S(1)}, ...), branch_computations={%region_0.1_spmd, %region_1.2_spmd, %region_2.3_spmd} | conditional | flops 12884901888 | bytes 75497640 | solution.py:527
  21.0 1.1 branch_1_fun.4
  22.1 18.7 %all_to_all.33.refs_1_ = f32[4,46,16,128]{3,2,1,0:T(8,128)S(1)} all-to-all(f32[4,46,16,128]{3,2,1,0:T(8,128)S(1)} %branch_1_fun.4), channel_id=1, replica_groups={{0,1,2,3},{4,5,6,7},{8,9,10,11},{12,13,14,15},{32,33,34,35},{36,37,38,3..., dimensions={0} | all-to-all | bytes 3014656 | tf_op jit(solution)/shard_map/cond/branch_1_fun/all_to_all | solution.py:93
  40.9 1.3 collective-permute-start.5
  42.2 1.4 collective-permute-start.4
  43.6 6.3 %branch_1_fun.5.refs_4_ = f32[8,1024,128]{2,1,0:T(8,128)S(1)} custom-call(s32[128]{0:T(128)S(1)} %get-tuple-element.31.plan_ref, bf16[4,4,2,1024,128]{4,3,2,1,0:T(8,128)(2,1)S(1)} %get-tuple-element.32.refs_0_.refs_1_, f32[4,46,16,128]{3,2,1,0:T(8,128)S(1)} %all_to_all.33.refs_1_), custom_call_target="tpu_custom_call" | custom-call | flops 3221225472 | bytes 12582912 | tf_op jit(solution)/shard_map/cond/branch_1_fun/pallas_call | solution.py:326
  49.9 11.1 %collective-permute-done.5.refs_3_ = f32[4,46,16,128]{3,2,1,0:T(8,128)S(1)} collective-permute-done((f32[4,46,16,128]{3,2,1,0:T(8,128)S(1)}, f32[4,46,16,128]{3,2,1,0:T(8,128)S(1)}, u32[]{:S(2)}, u32[]{:S(2)}) %collective-permute-start.5) | collective-permute-done | bytes 1507360 | tf_op jit(solution)/shard_map/cond/branch_1_fun/ppermute | solution.py:84
  61.0 0.1 collective-permute-done.4.refs_2_
  61.0 0.1 slice.21
  61.1 0.1 slice.20
  61.1 2.5 %collective-permute-start.6 = (f32[2,46,16,128]{3,2,1,0:T(8,128)S(1)}, f32[2,46,16,128]{3,2,1,0:T(8,128)S(1)}, u32[]{:S(2)}, u32[]{:S(2)}) collective-permute-start(f32[2,46,16,128]{3,2,1,0:T(8,128)S(1)} %slice.20), channel_id=1, source_target_pairs={{4,0},{5,1},{6,2},{7,3},{8,4},{9,5},{10,6},{11,7},{12,8},{13,9},{1... | collective-permute-start | bytes 2261000 | tf_op jit(solution)/shard_map/cond/branch_1_fun/ppermute | solution.py:84
  63.7 10.8 %branch_1_fun.6.refs_3_ = f32[8,1024,128]{2,1,0:T(8,128)S(1)} custom-call(s32[128]{0:T(128)S(1)} %get-tuple-element.31.plan_ref, bf16[4,4,2,1024,128]{4,3,2,1,0:T(8,128)(2,1)S(1)} %get-tuple-element.32.refs_0_.refs_1_, bf16[4,4,2,1024,128]{4,3,2,1,0:T(8,128)(2,1)S(1)} %get-tuple-element.32.refs_0_.refs_1_, ...), custom_call_target="tpu_custom_call" | custom-call | flops 6442450944 | bytes 12582912 | tf_op jit(solution)/shard_map/cond/branch_1_fun/pallas_call | solution.py:326
  74.5 1.1 collective-permute-done.7.refs_2_
  75.7 6.7 %branch_1_fun.7 = (f32[2,1024,128]{2,1,0:T(8,128)S(1)}, f32[2,1024,128]{2,1,0:T(8,128)}, f32[2,1024,128]{2,1,0:T(8,128)}, f32[2,1024,128]{2,1,0:T(8,128)}) custom-call(s32[128]{0:T(128)S(1)} %get-tuple-element.31.plan_ref, bf16[4,4,2,1024,128]{4,3,2,1,0:T(8,128)(2,1)S(1)} %get-tuple-element.32.refs_0_.refs_1_, ...), custom_call_target="tpu_custom_call" | custom-call | flops 3221225472 | bytes 12582912 | tf_op jit(solution)/shard_map/cond/branch_1_fun/pallas_call | solution.py:326
  82.3 3.6 %collective-permute-start.15 = (f32[2,1024,128]{2,1,0:T(8,128)}, f32[2,1024,128]{2,1,0:T(8,128)S(1)}, u32[]{:S(2)}, u32[]{:S(2)}) collective-permute-start(f32[2,1024,128]{2,1,0:T(8,128)} %get-tuple-element.92), channel_id=1, source_target_pairs={{16,0},{17,1},{18,2},{19,3},{20,4},{21,5},{22,6},{23,7},{24,8},{25... | collective-permute-start | bytes 3145736 | tf_op jit(solution)/shard_map/ppermute | solution.py:89
  85.9 0.1 collective-permute-start.14
  86.0 2.4 %collective-permute-done.15 = f32[2,1024,128]{2,1,0:T(8,128)S(1)} collective-permute-done((f32[2,1024,128]{2,1,0:T(8,128)}, f32[2,1024,128]{2,1,0:T(8,128)S(1)}, u32[]{:S(2)}, u32[]{:S(2)}) %collective-permute-start.15) | collective-permute-done | bytes 1048608 | tf_op jit(solution)/shard_map/ppermute | solution.py:89
  88.4 1.3 add.19
  89.8 2.0 %collective-permute-start.16 = (f32[2,1024,128]{2,1,0:T(8,128)S(1)}, f32[2,1024,128]{2,1,0:T(8,128)S(1)}, u32[]{:S(2)}, u32[]{:S(2)}) collective-permute-start(f32[2,1024,128]{2,1,0:T(8,128)S(1)} %add.19), channel_id=1, source_target_pairs={{32,0},{33,1},{34,2},{35,3},{36,4},{37,5},{38,6},{39,7},{40,8},{41... | collective-permute-start | bytes 3145736 | tf_op jit(solution)/shard_map/ppermute | solution.py:72
  91.7 3.3 %shard_map.131 = (bf16[640,1024]{1,0:T(8,128)(2,1)S(1)}, bf16[640,1024]{1,0:T(8,128)(2,1)S(1)}) custom-call(s32[128]{0:T(128)S(1)} %shard_map.128.plan_ref, f32[1024,512]{1,0:T(8,128)S(1)} %copy-done, f32[1024,512]{1,0:T(8,128)} %child_ref.2), custom_call_target="tpu_custom_call" | custom-call | flops 1048576 | bytes 8388608 | tf_op jit(solution)/shard_map/pallas_call | solution.py:384
  95.0 0.1 add.18
  95.1 9.6 %collective-permute-done.16 = f32[2,1024,128]{2,1,0:T(8,128)S(1)} collective-permute-done((f32[2,1024,128]{2,1,0:T(8,128)S(1)}, f32[2,1024,128]{2,1,0:T(8,128)S(1)}, u32[]{:S(2)}, u32[]{:S(2)}) %collective-permute-start.16) | collective-permute-done | bytes 1048608 | tf_op jit(solution)/shard_map/ppermute | solution.py:72
  104.7 0.1 add.20
  104.8 0.1 slice_bitcast_fusion
  104.9 0.6 collective-permute-start.17
  105.5 7.8 %collective-permute-done.17.passed_ref = f32[1024,128]{1,0:T(8,128)S(1)} collective-permute-done((f32[1024,128]{1,0:T(8,128)S(1)}, f32[1024,128]{1,0:T(8,128)S(1)}, u32[]{:S(2)}, u32[]{:S(2)}) %collective-permute-start.17) | collective-permute-done | bytes 524320 | tf_op jit(solution)/shard_map/ppermute | solution.py:72
  113.3 1.2 shard_map.132
  114.5 0.6 collective-permute-start.18
  115.1 8.2 %all_to_all.35 = f32[4,160,128]{2,1,0:T(8,128)S(1)} all-to-all(f32[4,160,128]{2,1,0:T(8,128)S(1)} %bitcast.16), channel_id=1, replica_groups={{0,1,2,3},{4,5,6,7},{8,9,10,11},{12,13,14,15},{32,33,34,35},{36,37,38,3..., dimensions={0} | all-to-all | bytes 655360 | tf_op jit(solution)/shard_map/all_to_all | solution.py:93
  123.4 0.1 pad_maximum_fusion.own_a
  123.5 5.2 %collective-permute-start.20 = (f32[2,1024,128]{2,1,0:T(8,128)S(1)}, f32[2,1024,128]{2,1,0:T(8,128)S(1)}, u32[]{:S(2)}, u32[]{:S(2)}) collective-permute-start(f32[2,1024,128]{2,1,0:T(8,128)S(1)} %pad_maximum_fusion.own_a), channel_id=1, source_target_pairs={{16,0},{17,1},{18,2},{19,3},{20,4},{21,5},{22,6},{23,7},{24,8},{25... | collective-permute-start | bytes 3145736 | tf_op jit(solution)/shard_map/ppermute | solution.py:89
  128.7 0.8 collective-permute-start.19
  129.5 8.3 %all_to_all.36 = f32[4,160,128]{2,1,0:T(8,128)S(1)} all-to-all(f32[4,160,128]{2,1,0:T(8,128)S(1)} %broadcast_in_dim.6), channel_id=1, replica_groups={{0,4,8,12},{1,5,9,13},{2,6,10,14},{3,7,11,15},{32,36,40,44},{33,37,41,4..., dimensions={0} | all-to-all | bytes 655360 | tf_op jit(solution)/shard_map/all_to_all | solution.py:93
  137.9 8.9 %all_to_all.37 = f32[4,160,128]{2,1,0:T(8,128)S(1)} all-to-all(f32[4,160,128]{2,1,0:T(8,128)S(1)} %broadcast_in_dim.7), channel_id=1, replica_groups={{0,32,64,96},{1,33,65,97},{2,34,66,98},{3,35,67,99},{4,36,68,100},{5,37..., dimensions={0} | all-to-all | bytes 655360 | tf_op jit(solution)/shard_map/all_to_all | solution.py:93
  146.8 2.4 %collective-permute-start.21 = (f32[2,1024,128]{2,1,0:T(8,128)S(1)}, f32[2,1024,128]{2,1,0:T(8,128)S(1)}, u32[]{:S(2)}, u32[]{:S(2)}) collective-permute-start(f32[2,1024,128]{2,1,0:T(8,128)S(1)} %collective-permute-done.19.own_b), channel_id=1, source_target_pairs={{16,0},{17,1},{18,2},{19,3},{20,4},{21,5},{22,6},{23,7},{24,8},{25... | collective-permute-start | bytes 3145736 | tf_op jit(solution)/shard_map/ppermute | solution.py:89
  149.2 0.1 broadcast_in_dim.8
  149.3 13.8 %all_to_all.38.own_ref = f32[4,4,160,128]{3,2,1,0:T(8,128)S(1)} all-to-all(f32[4,4,160,128]{3,2,1,0:T(8,128)S(1)} %broadcast_in_dim.8), channel_id=1, replica_groups={{0,1,2,3},{4,5,6,7},{8,9,10,11},{12,13,14,15},{32,33,34,35},{36,37,38,3..., dimensions={0} | all-to-all | bytes 2621440 | tf_op jit(solution)/shard_map/all_to_all | solution.py:93
  163.1 1.2 collective-permute-start.22
  164.3 4.9 %shard_map.133 = (f32[1024,512]{1,0:T(8,128)}, f32[1024,512]{1,0:T(8,128)}) custom-call(s32[128]{0:T(128)S(1)} %copy-done.5, f32[2,1024,128]{2,1,0:T(8,128)S(1)} %pad_maximum_fusion.own_a, f32[2,1024,128]{2,1,0:T(8,128)S(1)} %collective-permute-done.19.own_b, f32[2,1024,128]{2,1,0:T(8,128)S(1)} %collective-permute-done.20.other_a, ...), custom_call_target="tpu_custom_call" | custom-call | flops 1610612736 | bytes 8388608 | tf_op jit(solution)/shard_map/pallas_call | solution.py:453
  169.2 4.5 %shard_map.134 = (f32[512,512]{1,0:T(8,128)}, f32[512,512]{1,0:T(8,128)}, f32[512,512]{1,0:T(8,128)}) custom-call(s32[128]{0:T(128)S(1)} %copy-done.5, f32[4,4,160,128]{3,2,1,0:T(8,128)S(1)} %all_to_all.38.own_ref, f32[4,4,160,128]{3,2,1,0:T(8,128)S(1)} %collective-permute-done.22.other_ref, f32[512,512]{1,0:T(8,128)S(1)} %copy-done.1, ...), custom_call_target="tpu_custom_call" | custom-call | flops 2415919104 | bytes 10485760 | tf_op jit(solution)/shard_map/pallas_call | solution.py:500
  (24 shorter events, 0.1 us)
Async XLA Ops:
  4.4 16.5 %collective-permute-start.12 = (f32[2,4,16,512]{3,2,1,0:T(8,128)}, f32[2,4,16,512]{3,2,1,0:T(8,128)S(1)}, u32[]{:S(2)}, u32[]{:S(2)}) collective-permute-start(f32[2,4,16,512]{3,2,1,0:T(8,128)} %get-tuple-element.83), channel_id=1, source_target_pairs={{0,0},{16,1},{1,2},{17,3},{32,4},{48,5},{33,6},{49,7},{64,8},{80,9... | collective-permute-start | bytes 786440 | tf_op jit(solution)/shard_map/ppermute | solution.py:524
  8.9 12.0 %collective-permute-start.13 = (f32[2,4,16,512]{3,2,1,0:T(8,128)}, f32[2,4,16,512]{3,2,1,0:T(8,128)S(1)}, u32[]{:S(2)}, u32[]{:S(2)}) collective-permute-start(f32[2,4,16,512]{3,2,1,0:T(8,128)} %get-tuple-element.84), channel_id=1, source_target_pairs={{1,0},{17,1},{0,2},{16,3},{33,4},{49,5},{32,6},{48,7},{65,8},{81,9... | collective-permute-start | bytes 786440 | tf_op jit(solution)/shard_map/ppermute | solution.py:524
  15.2 76.5 %copy-start.4 = (s32[128]{0:T(128)}, s32[128]{0:T(128)S(1)}, u32[]{:S(2)}) copy-start(s32[128]{0:T(128)S(1)} %shard_map.128.plan_ref) | copy-start | bytes 1540
  40.9 20.1 %collective-permute-start.5 = (f32[4,46,16,128]{3,2,1,0:T(8,128)S(1)}, f32[4,46,16,128]{3,2,1,0:T(8,128)S(1)}, u32[]{:S(2)}, u32[]{:S(2)}) collective-permute-start(f32[4,46,16,128]{3,2,1,0:T(8,128)S(1)} %all_to_all.33.refs_1_), channel_id=1, source_target_pairs={{12,0},{13,1},{14,2},{15,3},{0,4},{1,5},{2,6},{3,7},{4,8},{5,9},{6... | collective-permute-start | bytes 4521992 | tf_op jit(solution)/shard_map/cond/branch_1_fun/ppermute | solution.py:84
  42.2 18.9 %collective-permute-start.4 = (f32[4,46,16,128]{3,2,1,0:T(8,128)S(1)}, f32[4,46,16,128]{3,2,1,0:T(8,128)S(1)}, u32[]{:S(2)}, u32[]{:S(2)}) collective-permute-start(f32[4,46,16,128]{3,2,1,0:T(8,128)S(1)} %all_to_all.33.refs_1_), channel_id=1, source_target_pairs={{4,0},{5,1},{6,2},{7,3},{8,4},{9,5},{10,6},{11,7},{12,8},{13,9},{1... | collective-permute-start | bytes 4521992 | tf_op jit(solution)/shard_map/cond/branch_1_fun/ppermute | solution.py:84
  61.1 13.4 %collective-permute-start.6 = (f32[2,46,16,128]{3,2,1,0:T(8,128)S(1)}, f32[2,46,16,128]{3,2,1,0:T(8,128)S(1)}, u32[]{:S(2)}, u32[]{:S(2)}) collective-permute-start(f32[2,46,16,128]{3,2,1,0:T(8,128)S(1)} %slice.20), channel_id=1, source_target_pairs={{4,0},{5,1},{6,2},{7,3},{8,4},{9,5},{10,6},{11,7},{12,8},{13,9},{1... | collective-permute-start | bytes 2261000 | tf_op jit(solution)/shard_map/cond/branch_1_fun/ppermute | solution.py:84
  63.7 12.0 %collective-permute-start.7 = (f32[2,46,16,128]{3,2,1,0:T(8,128)S(1)}, f32[2,46,16,128]{3,2,1,0:T(8,128)S(1)}, u32[]{:S(2)}, u32[]{:S(2)}) collective-permute-start(f32[2,46,16,128]{3,2,1,0:T(8,128)S(1)} %slice.21), channel_id=1, source_target_pairs={{12,0},{13,1},{14,2},{15,3},{0,4},{1,5},{2,6},{3,7},{4,8},{5,9},{6... | collective-permute-start | bytes 2261000 | tf_op jit(solution)/shard_map/cond/branch_1_fun/ppermute | solution.py:84
  82.3 9.4 %copy-start = (f32[1024,512]{1,0:T(8,128)S(1)}, f32[1024,512]{1,0:T(8,128)}, u32[]{:S(2)}) copy-start(f32[1024,512]{1,0:T(8,128)} %parent_ref.2) | copy-start | bytes 6291460
  82.3 6.1 %collective-permute-start.15 = (f32[2,1024,128]{2,1,0:T(8,128)}, f32[2,1024,128]{2,1,0:T(8,128)S(1)}, u32[]{:S(2)}, u32[]{:S(2)}) collective-permute-start(f32[2,1024,128]{2,1,0:T(8,128)} %get-tuple-element.92), channel_id=1, source_target_pairs={{16,0},{17,1},{18,2},{19,3},{20,4},{21,5},{22,6},{23,7},{24,8},{25... | collective-permute-start | bytes 3145736 | tf_op jit(solution)/shard_map/ppermute | solution.py:89
  85.9 9.1 %collective-permute-start.14 = (f32[2,1024,128]{2,1,0:T(8,128)}, f32[2,1024,128]{2,1,0:T(8,128)S(1)}, u32[]{:S(2)}, u32[]{:S(2)}) collective-permute-start(f32[2,1024,128]{2,1,0:T(8,128)} %get-tuple-element.90), channel_id=1, source_target_pairs={{16,0},{17,1},{18,2},{19,3},{20,4},{21,5},{22,6},{23,7},{24,8},{25... | collective-permute-start | bytes 3145736 | tf_op jit(solution)/shard_map/ppermute | solution.py:89
  89.8 14.9 %collective-permute-start.16 = (f32[2,1024,128]{2,1,0:T(8,128)S(1)}, f32[2,1024,128]{2,1,0:T(8,128)S(1)}, u32[]{:S(2)}, u32[]{:S(2)}) collective-permute-start(f32[2,1024,128]{2,1,0:T(8,128)S(1)} %add.19), channel_id=1, source_target_pairs={{32,0},{33,1},{34,2},{35,3},{36,4},{37,5},{38,6},{39,7},{40,8},{41... | collective-permute-start | bytes 3145736 | tf_op jit(solution)/shard_map/ppermute | solution.py:72
  104.9 8.4 %collective-permute-start.17 = (f32[1024,128]{1,0:T(8,128)S(1)}, f32[1024,128]{1,0:T(8,128)S(1)}, u32[]{:S(2)}, u32[]{:S(2)}) collective-permute-start(f32[1024,128]{1,0:T(8,128)S(1)} %get-tuple-element.116), channel_id=1, source_target_pairs={{96,0},{97,1},{98,2},{99,3},{100,4},{101,5},{102,6},{103,7},{104,8... | collective-permute-start | bytes 1572872 | tf_op jit(solution)/shard_map/ppermute | solution.py:72
  114.5 8.9 %collective-permute-start.18 = (f32[1024,128]{1,0:T(8,128)S(1)}, f32[1024,128]{1,0:T(8,128)S(1)}, u32[]{:S(2)}, u32[]{:S(2)}) collective-permute-start(f32[1024,128]{1,0:T(8,128)S(1)} %get-tuple-element.99), channel_id=1, source_target_pairs={{96,0},{97,1},{98,2},{99,3},{100,4},{101,5},{102,6},{103,7},{104,8... | collective-permute-start | bytes 1572872 | tf_op jit(solution)/shard_map/ppermute | solution.py:72
  123.5 23.3 %collective-permute-start.20 = (f32[2,1024,128]{2,1,0:T(8,128)S(1)}, f32[2,1024,128]{2,1,0:T(8,128)S(1)}, u32[]{:S(2)}, u32[]{:S(2)}) collective-permute-start(f32[2,1024,128]{2,1,0:T(8,128)S(1)} %pad_maximum_fusion.own_a), channel_id=1, source_target_pairs={{16,0},{17,1},{18,2},{19,3},{20,4},{21,5},{22,6},{23,7},{24,8},{25... | collective-permute-start | bytes 3145736 | tf_op jit(solution)/shard_map/ppermute | solution.py:89
  128.7 18.1 %collective-permute-start.19 = (f32[2,1024,128]{2,1,0:T(8,128)S(1)}, f32[2,1024,128]{2,1,0:T(8,128)S(1)}, u32[]{:S(2)}, u32[]{:S(2)}) collective-permute-start(f32[2,1024,128]{2,1,0:T(8,128)S(1)} %pad_maximum_fusion.own_a), channel_id=1, source_target_pairs={{32,0},{33,1},{34,2},{35,3},{36,4},{37,5},{38,6},{39,7},{40,8},{41... | collective-permute-start | bytes 3145736 | tf_op jit(solution)/shard_map/ppermute | solution.py:72
  146.8 17.5 %copy-start.1 = (f32[512,512]{1,0:T(8,128)S(1)}, f32[512,512]{1,0:T(8,128)}, u32[]{:S(2)}) copy-start(f32[512,512]{1,0:T(8,128)} %cross_ref.3) | copy-start | bytes 3145732
  146.8 17.5 %copy-start.5 = (s32[128]{0:T(128)S(1)}, s32[128]{0:T(128)}, u32[]{:S(2)}) copy-start(s32[128]{0:T(128)} %copy-done.4) | copy-start | bytes 1540
  146.8 16.3 %collective-permute-start.21 = (f32[2,1024,128]{2,1,0:T(8,128)S(1)}, f32[2,1024,128]{2,1,0:T(8,128)S(1)}, u32[]{:S(2)}, u32[]{:S(2)}) collective-permute-start(f32[2,1024,128]{2,1,0:T(8,128)S(1)} %collective-permute-done.19.own_b), channel_id=1, source_target_pairs={{16,0},{17,1},{18,2},{19,3},{20,4},{21,5},{22,6},{23,7},{24,8},{25... | collective-permute-start | bytes 3145736 | tf_op jit(solution)/shard_map/ppermute | solution.py:89
  163.1 6.1 %copy-start.2 = (f32[512,512]{1,0:T(8,128)S(1)}, f32[512,512]{1,0:T(8,128)}, u32[]{:S(2)}) copy-start(f32[512,512]{1,0:T(8,128)} %parent_ref.3) | copy-start | bytes 3145732
  163.1 6.1 %copy-start.3 = (f32[512,512]{1,0:T(8,128)S(1)}, f32[512,512]{1,0:T(8,128)}, u32[]{:S(2)}) copy-start(f32[512,512]{1,0:T(8,128)} %child_ref.3) | copy-start | bytes 3145732
  163.1 6.1 %collective-permute-start.22 = (f32[4,4,160,128]{3,2,1,0:T(8,128)S(1)}, f32[4,4,160,128]{3,2,1,0:T(8,128)S(1)}, u32[]{:S(2)}, u32[]{:S(2)}) collective-permute-start(f32[4,4,160,128]{3,2,1,0:T(8,128)S(1)} %all_to_all.38.own_ref), channel_id=1, source_target_pairs={{16,0},{17,1},{18,2},{19,3},{20,4},{21,5},{22,6},{23,7},{24,8},{25... | collective-permute-start | bytes 3932168 | tf_op jit(solution)/shard_map/ppermute | solution.py:89
